TPU v7x, 32 devices: a whole 2x2x4 slice. The times are simulated.
32 devices in a mesh: dp: 16 (over z, x, core), tensor: 2 (over y).
Axes of the slice: x: 2, y: 2, z: 4, core: 2. Of those that a mesh axis runs over, the one named last changes fastest.
Arguments:
- block_input: bfloat16 [16384, 1536], P('dp'), may hold values from -6 to 6
- norm_gain: float32 [1536], replicated, may hold values from 0.5 to 1.5
- z_weight: bfloat16 [1536, 3072], P(None, 'tensor'), may hold values from -0.15625 to 0.15625
- x_weight: bfloat16 [1536, 3072], P(None, 'tensor'), may hold values from -0.15625 to 0.15625
- bc_weight: bfloat16 [1536, 256], replicated, may hold values from -0.15625 to 0.15625
- dt_weight: bfloat16 [1536, 48], P(None, 'tensor'), may hold values from -0.15625 to 0.15625
- x_conv: float32 [4, 3072], P(None, 'tensor'), may hold values from -0.5 to 0.5
- x_conv_bias: float32 [3072], P('tensor'), may hold values from -0.5 to 0.5
- bc_conv: float32 [4, 256], replicated, may hold values from -0.5 to 0.5
- bc_conv_bias: float32 [256], replicated, may hold values from -0.5 to 0.5
- dt_bias: float32 [48], P('tensor'), may hold values from -7 to -2.3
- a_log: float32 [48], P('tensor'), may hold values from 0 to 2.77
- d_skip: float32 [48], P('tensor'), may hold values from 0.5 to 1.5
- gated_gain: float32 [3072], P('tensor'), may hold values from 0.5 to 1.5
- out_weight: bfloat16 [3072, 1536], P('tensor'), may hold values from -0.109375 to 0.109375
- out_cotangent: bfloat16 [16384, 1536], P('dp'), may hold values from -6 to 6
Outputs:
- block_output: bfloat16 [16384, 1536], P('dp')
- input_grad: bfloat16 [16384, 1536], P('dp')
- norm_gain_grad: float32 [1536], P(('dp', 'tensor'))
- z_weight_grad: float32 [1536, 3072], P('dp', 'tensor')
- x_weight_grad: float32 [1536, 3072], P('dp', 'tensor')
- bc_weight_grad: float32 [1536, 256], P(('dp', 'tensor'))
- dt_weight_grad: float32 [1536, 48], P('dp', 'tensor')
- x_conv_grad: float32 [4, 3072], P(None, 'tensor')
- x_conv_bias_grad: float32 [3072], P('tensor')
- bc_conv_grad: float32 [4, 256], P(None, ('dp', 'tensor'))
- bc_conv_bias_grad: float32 [256], P(('dp', 'tensor'))
- dt_bias_grad: float32 [48], P('tensor')
- a_log_grad: float32 [48], P('tensor')
- d_skip_grad: float32 [48], P('tensor')
- gated_gain_grad: float32 [3072], P('tensor')
- out_weight_grad: float32 [3072, 1536], P('tensor', 'dp')
All inputs are finite; a program needn't handle non-finite values.
Results may differ from a plain program's by a relative error of at most 0.0076.
Values sent between devices are 32-bit elements; how exact they have to be, the bound alone decides.
No kernel may reach another device: no remote copies, remote signals or barrier semaphores. Data moves between devices by JAX's collectives and lax.ppermute only.
A program may use at most 256 MiB of HBM per device.

v0:
```python
import functools
import math

import jax
import jax.numpy as jnp
from jax import lax
from jax.experimental import pallas as pl
from jax.experimental.pallas import tpu as pltpu
from jax.sharding import PartitionSpec as P

SPAN = 256
LEN = 1024
EPS = 1e-05
HIGH = lax.Precision.HIGHEST
LOG2E = math.log2(math.e)
F32 = jnp.float32
BF16 = jnp.bfloat16
HALO = 8
GROUP = 32
VMEM = 56 * 1024 * 1024


class Named(dict):
    __getattr__ = dict.get
    __setattr__ = dict.__setitem__


def mm(a, b):
    return lax.dot_general(a, b, (((1,), (0,)), ((), ())), preferred_element_type=F32)


def mm_nt(a, b):
    return lax.dot_general(a, b, (((1,), (1,)), ((), ())), preferred_element_type=F32)


def mm_tn(a, b):
    return lax.dot_general(a, b, (((0,), (0,)), ((), ())), preferred_element_type=F32)


def split3(x):
    hi = x.astype(BF16)
    rest = x - hi.astype(F32)
    mid = rest.astype(BF16)
    low = (rest - mid.astype(F32)).astype(BF16)
    return hi, mid, low


def split2(x):
    hi = x.astype(BF16)
    return hi, (x - hi.astype(F32)).astype(BF16)


def side(a, b):
    return jnp.concatenate((a, b), axis=1)


def folded(x):
    half = x.shape[1] // 2
    return x[:, :half] + x[:, half:]


def fine_nn(left_pair, b):
    bh, bl = split2(b)
    depth = b.shape[0]
    return mm(left_pair, jnp.concatenate((bh, bh), axis=0)) + mm(left_pair[:, :depth], bl)


def fine_rows(left_stack, b):
    bh, bl = split2(b)
    rows = left_stack.shape[0] // 2
    both = mm(left_stack, bh)
    return both[:rows] + both[rows:] + mm(left_stack[:rows], bl)


def fine_nt(a, b):
    ah, al = split2(a)
    bh, bl = split2(b)
    return folded(mm_nt(ah, jnp.concatenate((bh, bl), axis=0))) + mm_nt(al, bh)


def iota(shape, axis):
    return lax.broadcasted_iota(jnp.int32, shape, axis)


def times_transposed(left, right):
    return lax.dot_general(left, right, (((1,), (1,)), ((), ())), preferred_element_type=F32)


def softplus(v):
    return jnp.maximum(v, 0.0) + jnp.log1p(jnp.exp(-jnp.abs(v)))


def three_parts(x):
    hi, mid, low = split3(x)
    lane = iota(x.shape, 1)
    parts = jnp.where(
        lane < GROUP, hi.astype(F32), jnp.where(lane < 2 * GROUP, mid.astype(F32), low.astype(F32))
    )
    return parts.astype(BF16)


def spread_matrix(block, heads, head_dim, lanes):
    shape = (lanes, heads * head_dim)
    row, col = iota(shape, 0), iota(shape, 1)
    head = block * heads + col // head_dim
    hit = (row == head) | (row == head + GROUP) | (row == head + 2 * GROUP)
    return jnp.where(hit, 1.0, 0.0).astype(BF16)


def gather_matrix(block, heads, head_dim, lanes):
    shape = (heads * head_dim, lanes)
    row, col = iota(shape, 0), iota(shape, 1)
    return jnp.where(col == block * heads + row // head_dim, 1.0, 0.0).astype(BF16)


def triangle(n, lower):
    row, col = iota((n, n), 0), iota((n, n), 1)
    return jnp.where(row >= col if lower else row <= col, 1.0, 0.0)


def pair_masks(head_dim):
    lane = iota((1, 4 * head_dim), 1) // head_dim % 2
    return [jnp.where(lane == k, 1.0, 0.0).astype(BF16) for k in range(2)]


def pair_parts(parts, head_dim, pair):
    at = slice(2 * pair * head_dim, 2 * (pair + 1) * head_dim)
    return side(parts[0][:, at], parts[1][:, at])


def earlier(x, halo, by):
    if by == 0:
        return x
    rolled = pltpu.roll(x, by, 0)
    head = iota((HALO, x.shape[1]), 0) < by
    front = pltpu.roll(halo, by, 0) if halo is not None else 0.0
    return jnp.concatenate((jnp.where(head, front, rolled[:HALO]), rolled[HALO:]), axis=0)


def later(x, halo, by):
    if by == 0:
        return x
    rows = x.shape[0]
    rolled = pltpu.roll(x, rows - by, 0)
    tail = iota((HALO, x.shape[1]), 0) >= HALO - by
    back = pltpu.roll(halo, HALO - by, 0) if halo is not None else 0.0
    end = jnp.where(tail, back, rolled[rows - HALO :])
    return jnp.concatenate((rolled[: rows - HALO], end), axis=0)


def conv_of(x, halo, taps, bias):
    count = taps.shape[0]
    shifted = [earlier(x, halo, count - 1 - k) for k in range(count)]
    total = bias + taps[0:1] * shifted[0]
    for k in range(1, count):
        total = total + taps[k : k + 1] * shifted[k]
    return total, shifted


def conv_back(grad, halo, taps):
    count = taps.shape[0]
    total = taps[count - 1 : count] * grad
    for k in range(count - 1):
        total = total + taps[k : k + 1] * later(grad, halo, count - 1 - k)
    return total


def unpacked(ref, taps):
    return ref[:taps], ref[taps : taps + 1], ref[taps + 1 : taps + 2], ref[taps + 2 : taps + 3]


def maybe(ref):
    return None if ref is None else ref[...]


def silu_slope(v, s):
    return s + v * s * (1.0 - s)


def triangle_sum(x, lower):
    lanes = x.shape[1]
    parts = mm(triangle(x.shape[0], lower).astype(BF16), jnp.concatenate(split3(x), axis=1))
    return parts[:, :lanes] + parts[:, lanes : 2 * lanes] + parts[:, 2 * lanes :]


def steps_of(dt_pre, dt_bias_ref, a_log_ref):
    dt = softplus(dt_pre + dt_bias_ref[...])
    decay = -jnp.exp(a_log_ref[...])
    rates = dt * (decay * LOG2E)
    cum = triangle_sum(rates, True)
    return dt, decay, cum


def row_sums(x):
    lanes = 128
    part = x[:, :lanes]
    for at in range(lanes, x.shape[1], lanes):
        part = part + x[:, at : at + lanes]
    return jnp.sum(part.T, axis=0, keepdims=True)


PIECE = 32


def slot_of(rel, n):
    bits = n.bit_length() - 1
    p = sum((rel >> b & 1) << (bits - 1 - b) for b in range(1, bits))
    first, half, quarter = rel & 1, n // 2, n // 4
    return jnp.where(first == 1, p, jnp.where(p >= quarter, half + p - quarter, n - quarter + p))


def arrange_rows(start, n, place, turned, target):
    block = target.shape[0] // n
    if n == 1 or block % PIECE:
        target[pl.ds(pl.multiple_of(start, PIECE), turned.shape[0]), :] = turned
        return
    for at in range(0, turned.shape[0], PIECE):
        begin = start + at
        owner = lax.div(begin, block)
        slot = slot_of(owner ^ place[0], n)
        to = pl.multiple_of(slot * block + begin - owner * block, PIECE)
        target[pl.ds(to, PIECE), :] = turned[at : at + PIECE]


def fwd_kernel(first, heads, head_dim, blocks, n_dp, refs):
    j = pl.program_id(0)
    r = refs
    rows = r.normed.shape[0]
    half = rows // 2
    states = r.bc_pre.shape[1] // 2
    lanes = r.dt_pre.shape[1]

    @pl.when(j == 0)
    def _():
        bc_pre = r.bc_pre[...]
        u, _ = conv_of(bc_pre, maybe(r.bc_halo), r.bc_conv[...], r.bc_conv_bias[...])
        act = u * jax.nn.sigmoid(u)
        b, c = act[:, :states], act[:, states:]
        r.cb[...] = side(*split2(c))
        r.bt[...] = jnp.concatenate(split2(b.T), axis=0)
        r.scores[...] = fine_nt(c, b) * triangle(rows, True)
        dt, decay, cum = steps_of(r.dt_pre[...], r.dt_bias, r.a_log)
        r.cum_t[...] = cum.T
        r.parts[0:rows, :] = three_parts(cum)
        r.parts[rows : 2 * rows, :] = three_parts(dt)
        r.u_out[...] = jnp.zeros_like(r.u_out)
        r.acc[...] = jnp.zeros_like(r.acc)

    width = heads * head_dim
    xp, zp = r.x_pre[...], r.z_pre[...]
    gate = zp * jax.nn.sigmoid(zp)
    columns = r.normed.shape[1] // blocks
    here = pl.ds(pl.multiple_of(j * columns, columns), columns)
    turned = r.normed[:, here].T
    arrange_rows(j * columns, n_dp, r.place, turned, r.normed_t)
    r.cot_t[here, :] = r.cot[:, here].T
    taps = r.bc_conv.shape[0]
    conv, conv_bias, d_skip, gated_gain = unpacked(r.packed, taps)
    u, _ = conv_of(xp, maybe(r.x_halo), conv, conv_bias)
    xa = u * jax.nn.sigmoid(u)
    spread = mm(r.parts[...], spread_matrix(j, heads, head_dim, lanes))
    cum_e, dt_e = spread[:rows], spread[rows:]
    w = xa * dt_e
    last = cum_e[rows - 1 : rows, :]
    scaled = w * jnp.exp2(last - cum_e)
    masks = pair_masks(head_dim)
    parts = split2(w)
    empty = jnp.zeros((half, half), BF16)
    cols = []
    for pair in range(heads // 2):
        both = pair_parts(parts, head_dim, pair)
        total = 0.0
        for k in range(2):
            head = 2 * pair + k
            row = r.cum_t[pl.ds(j * heads + head, 1), :]
            col = cum_e[:, head * head_dim : head * head_dim + 1]
            m = jnp.exp2(jnp.minimum(col[:half] - row[:, :half], 0.0)) * r.scores[:half, :half]
            top = [side(part, empty) for part in split2(m)]
            m = jnp.exp2(jnp.minimum(col[half:] - row, 0.0)) * r.scores[half:, :]
            bot = split2(m)
            stack = jnp.concatenate((top[0], bot[0], top[1], bot[1]), axis=0)
            total = total + mm(stack, both * masks[k])
        cols.append(folded(total[:rows] + total[rows:]))
    y = side(*cols)
    if first:
        r.state_out[...] = fine_rows(r.bt[...], scaled)
    else:
        state = r.state[...]
        y = y + jnp.exp2(cum_e) * fine_nn(r.cb[...], state)
        r.state_out[...] = jnp.exp2(last) * state + fine_rows(r.bt[...], scaled)
    mixed = y + d_skip * xa
    r.mixed[...] = mixed
    gated = mixed * gate
    gain = gated * gated_gain
    r.u_out[...] += mm(gain.astype(BF16), r.out_w[...])
    r.acc[...] += gated * gated

    @pl.when(j == pl.num_programs(0) - 1)
    def _():
        r.sums[0:1, :] = row_sums(r.acc[...])
        r.sums[1:2, :] = row_sums(r.cot[...].astype(F32) * r.u_out[...])
        r.sums[2:HALO, :] = jnp.zeros((HALO - 2, rows), F32)


def row_scales(r, inner_total):
    sums = (r.sums[...] + r.sums_other[...]).T
    rms = lax.rsqrt(sums[:, 0:1] / inner_total + EPS)
    return rms, sums[:, 1:2] * rms / inner_total


def gate_kernel(inner_total, taps, width, r):
    rms, row_dot = row_scales(r, inner_total)
    for start in range(0, r.z_pre.shape[1], width):
        at = slice(start, start + width)
        mg = mm_nt(r.cot[...], r.out_w[at, :])
        r.mg[:, at] = mg
        zp, mixed = r.z_pre[:, at], r.mixed[:, at]
        gain = r.packed[taps + 2 : taps + 3, at]
        sz = jax.nn.sigmoid(zp)
        gated_unit = mixed * (zp * sz) * rms
        r.mixer_out[:, at] = (gated_unit * gain).astype(BF16)
        gg = rms * (mg * gain - gated_unit * row_dot)
        r.z_low[:, at] = (gg * mixed * silu_slope(zp, sz)).astype(BF16)


def output_kernel(inner_total, r):
    rms, _ = row_scales(r, inner_total)
    total = (r.share[...] + r.share_other[...]) * rms
    r.out[...] = (r.xin[...].astype(F32) + total).astype(BF16)


def grad_kernel(r):
    total = r.share[...] + r.share_other[...]
    r.out[...] = (r.cot[...].astype(F32) + total).astype(BF16)


def bwd_kernel(first, last_chunk, heads, head_dim, inner_total, refs):
    j = pl.program_id(0)
    r = refs
    rows = r.xin.shape[0]
    half = rows // 2
    states = r.bc_w.shape[1] // 2
    lanes = r.dt_w.shape[1]
    width = heads * head_dim
    taps = r.bc_conv.shape[0]
    conv, conv_bias, d_skip, gated_gain = unpacked(r.packed, taps)

    def column_sum(v):
        return jnp.sum(v, axis=0, keepdims=True)

    @pl.when(j == 0)
    def _():
        bc_pre = r.bc_pre[...]
        u, _ = conv_of(bc_pre, maybe(r.bc_halo), r.bc_conv[...], r.bc_conv_bias[...])
        s = jax.nn.sigmoid(u)
        act = u * s
        r.bc_slope[...] = silu_slope(u, s)
        b, c = act[:, :states], act[:, states:]
        r.bb[...] = side(*split2(b))
        r.cb[...] = side(*split2(c))
        r.ct[...] = jnp.concatenate(split2(c.T), axis=0)
        r.scores[...] = fine_nt(b, c) * triangle(rows, False)
        dt, decay, cum = steps_of(r.dt_pre[...], r.dt_bias, r.a_log)
        r.dt[...] = dt
        r.cum_t[...] = cum.T
        r.parts[0:rows, :] = three_parts(cum)
        r.parts[rows : 2 * rows, :] = three_parts(dt)
        r.x_low_before[...] = jnp.zeros_like(r.x_low_before)
        for ref in (r.d_scores, r.db, r.dc, r.d_cum, r.d_dt, r.ng):
            ref[...] = jnp.zeros_like(ref)
        rms, row_dot = row_scales(r, inner_total)
        r.rows[:, 0:1] = rms
        r.rows[:, 1:2] = row_dot

    xp = r.x_pre[...]
    u, shifted = conv_of(xp, maybe(r.x_halo), conv, conv_bias)
    su = jax.nn.sigmoid(u)
    xa = u * su
    spread = mm(r.parts[...], spread_matrix(j, heads, head_dim, lanes))
    cum_e, dt_e = spread[:rows], spread[rows:]
    w = xa * dt_e
    last = cum_e[rows - 1 : rows, :]
    rms, row_dot = r.rows[:, 0:1], r.rows[:, 1:2]
    zp, mg, mixed = r.z_pre[...], r.mg[...], r.mixed[...]
    sz = jax.nn.sigmoid(zp)
    gate = zp * sz
    y = mixed - d_skip * xa
    gated_unit = mixed * gate * rms
    gg = rms * (mg * gated_gain - gated_unit * row_dot)
    dy = gg * gate
    sums = [column_sum(mg * gated_unit), column_sum(dy * xa)]
    masks = pair_masks(head_dim)
    w_parts = split2(w)
    dy_parts = split2(dy)
    empty = jnp.zeros((half, half), BF16)
    cols = []
    for pair in range(heads // 2):
        at = slice(2 * pair * head_dim, 2 * (pair + 1) * head_dim)
        w_both = pair_parts(w_parts, head_dim, pair)
        w_high = w_parts[0][:, at]
        dy_both = pair_parts(dy_parts, head_dim, pair)
        dy_high = side(dy_parts[0][:, at], dy_parts[0][:, at])
        dy_low = dy_parts[1][:, at]
        total = 0.0
        for k in range(2):
            head = 2 * pair + k
            row = r.cum_t[pl.ds(j * heads + head, 1), :]
            col = cum_e[:, head * head_dim : head * head_dim + 1]
            dk, dk_high = dy_both * masks[k], dy_high * masks[k]
            dk_low = dy_low * masks[k][:, : 2 * head_dim]
            grad = mm_nt(w_both, dk_high) + mm_nt(w_high, dk_low)
            decay = jnp.exp2(jnp.minimum(row - col[:half], 0.0))
            r.d_scores[:half, :] += grad[:half] * decay
            top = split2(decay * r.scores[:half, :])
            decay = jnp.exp2(jnp.minimum(row[:, half:] - col[half:], 0.0))
            r.d_scores[half:, half:] += grad[half:, half:] * decay
            bot = [side(empty, part) for part in split2(decay * r.scores[half:, half:])]
            stack = jnp.concatenate((top[0], bot[0], top[1], bot[1]), axis=0)
            total = total + mm(stack, dk)
        cols.append(folded(total[:rows] + total[rows:]))
    dw = side(*cols)
    extra = None
    if not last_chunk:
        to_end = jnp.exp2(last - cum_e)
        d_state = r.d_state[...]
        ds = fine_nn(r.bb[...], d_state) * to_end
        r.db[...] += fine_nt(w * to_end, d_state)
        dw = dw + ds
        extra = column_sum(w * ds)
    if not first:
        state = r.state[...]
        g = jnp.exp2(cum_e) * dy
        r.dc[...] += fine_nt(g, state)
        d_state_out = fine_rows(r.ct[...], g)
        if not last_chunk:
            kept = jnp.exp2(last) * d_state
            extra = extra + column_sum(kept * state)
            d_state_out = d_state_out + kept
        r.d_state_out[...] = d_state_out
    q = dy * y - w * dw
    if extra is not None:
        q = q + jnp.where(iota((rows, 1), 0) == rows - 1, 1.0, 0.0) * extra
    gather = gather_matrix(j, heads, head_dim, lanes)
    stack = split3(q) + split2(dw * xa)
    given = mm(jnp.concatenate(stack, axis=0), gather)
    given = [given[at * rows : (at + 1) * rows] for at in range(5)]
    r.d_cum[...] += given[0] + given[1] + given[2]
    r.d_dt[...] += given[3] + given[4]
    du = (d_skip * dy + dw * dt_e) * silu_slope(u, su)
    xg = conv_back(du, maybe(r.du_halo), conv)
    r.du_halo_out[...] = du[:HALO, :]
    for k in range(taps):
        sums.append(column_sum(du * shifted[k]))
    sums.append(column_sum(du))
    for at, value in enumerate(sums):
        before = 0.0 if last_chunk else r.x_sums_in[at : at + 1, :]
        r.x_sums[at : at + 1, :] = value + before
    r.x_sums[len(sums) : HALO, :] = jnp.zeros((HALO - len(sums), width), F32)
    xl = xg.astype(BF16)
    r.x_low[...] = xl
    r.ng[...] += mm_nt(r.z_low[...], r.z_w[...]) + mm_nt(r.x_low_before[...], r.x_w[...])
    r.x_low_before[...] = xl

    @pl.when(j == pl.num_programs(0) - 1)
    def _():
        hi, low = split2(r.d_scores[...] * triangle(rows, False))
        cb, bb = r.cb[...], r.bb[...]
        db = r.db[...] + folded(mm(hi, cb)) + mm(low, cb[:, :states])
        dc = r.dc[...] + folded(mm_tn(hi, bb)) + mm_tn(low, bb[:, :states])
        d_rates = triangle_sum(r.d_cum[...], False)
        dt = r.dt[...]
        decay = -jnp.exp(r.a_log[...])
        d_dt = d_rates * decay + r.d_dt[...]
        dtg = d_dt * jax.nn.sigmoid(r.dt_pre[...] + r.dt_bias[...])
        dtl = jnp.where(iota(dtg.shape, 1) < GROUP, dtg, 0.0).astype(BF16)
        r.side_low[:, 2 * states :] = dtl
        head_sums = [column_sum(dtg), column_sum(d_rates * dt) * decay]
        for at, value in enumerate(head_sums):
            before = 0.0 if last_chunk else r.head_sums_in[at : at + 1, :]
            r.head_sums[at : at + 1, :] = value + before
        r.head_sums[2:HALO, :] = jnp.zeros((HALO - 2, lanes), F32)
        du_bc = jnp.concatenate((db, dc), axis=1) * r.bc_slope[...]
        bg = conv_back(du_bc, maybe(r.du_bc_halo), r.bc_conv[...])
        r.du_bc_halo_out[...] = du_bc[:HALO, :]
        bc_sums = []
        for k in range(taps):
            near = earlier(r.bc_pre[...], maybe(r.bc_halo), taps - 1 - k)
            bc_sums.append(column_sum(du_bc * near))
        bc_sums.append(column_sum(du_bc))
        for at, value in enumerate(bc_sums):
            before = 0.0 if last_chunk else r.bc_sums_in[at : at + 1, :]
            r.bc_sums[at : at + 1, :] = value + before
        r.bc_sums[len(bc_sums) : HALO, :] = jnp.zeros((HALO - len(bc_sums), 2 * states), F32)
        bl = bg.astype(BF16)
        r.side_low[:, : 2 * states] = bl
        ng = r.ng[...] + mm_nt(bl, r.bc_w[...]) + mm_nt(dtl, r.dt_w[...])
        ng = ng + mm_nt(xl, r.x_w_last[...])
        res = r.xin[...].astype(F32)
        inv = lax.rsqrt(jnp.mean(res * res, axis=1, keepdims=True) + EPS)
        unit = res * inv
        gain_sum = column_sum(ng * unit)
        r.gain_sums[0:1, :] = gain_sum if last_chunk else gain_sum + r.gain_sums_in[0:1, :]
        r.gain_sums[1:HALO, :] = jnp.zeros((HALO - 1, gain_sum.shape[1]), F32)
        iu = ng * r.norm_gain[...]
        r.in_part[...] = inv * (iu - unit * jnp.mean(iu * unit, axis=1, keepdims=True))


def run_kernel(body, grid, operands, outs, scratch, carried, waits=(), flops=1):
    names, arrays, specs = [], [], []
    for name, (array, block, index) in operands.items():
        names.append(name)
        arrays.append(array)
        whole = pl.BlockSpec(memory_space=pltpu.SMEM)
        specs.append(whole if block is None else pl.BlockSpec(block, index))
    aliases = {}
    out_names = list(outs)
    for at, name in enumerate(out_names):
        if name in carried:
            aliases[len(arrays)] = at
            names.append(name + "_old")
            arrays.append(carried[name])
            specs.append(pl.BlockSpec(memory_space=pl.ANY))
    for at, array in enumerate(waits):
        names.append(at)
        arrays.append(array)
        specs.append(pl.BlockSpec(memory_space=pl.ANY))
    scratch_names = list(scratch)

    def kernel(*refs):
        body(Named(zip(names + out_names + scratch_names, refs)))

    given = pl.pallas_call(
        kernel,
        grid=grid,
        in_specs=specs,
        out_specs=[pl.BlockSpec(block, index) for _, block, index in outs.values()],
        out_shape=[shape for shape, _, _ in outs.values()],
        scratch_shapes=[pltpu.VMEM(shape, kind) for shape, kind in scratch.values()],
        input_output_aliases=aliases,
        compiler_params=pltpu.CompilerParams(
            dimension_semantics=("arbitrary",) * len(grid), vmem_limit_bytes=VMEM
        ),
        cost_estimate=pl.CostEstimate(flops=flops, bytes_accessed=1, transcendentals=0),
    )(*arrays)
    return Named(zip(out_names, given))


def shape(*dims, kind=F32):
    return jax.ShapeDtypeStruct(dims, kind)


def relative_masks(n, flip):
    bits = n.bit_length() - 1
    masks = []
    for p in range(n // 2):
        masks.append(flip + sum((p >> (bits - 1 - b) & 1) << b for b in range(1, bits)))
    return masks


def arranged(left, n):
    if n == 1:
        return None, left, left[:0]
    block = left.shape[0] // n
    me = lax.axis_index("dp")
    if block % PIECE == 0:
        half, quarter = left.shape[0] // 2, left.shape[0] // 4
        return left[:half], left[half : half + quarter], left[half + quarter :]

    def pick(masks):
        rows = [lax.dynamic_slice_in_dim(left, (me ^ mask) * block, block, 0) for mask in masks]
        return jnp.concatenate(rows, axis=0)

    kept = relative_masks(n, 0)
    half = len(kept) // 2
    if not half:
        return pick(relative_masks(n, 1)), pick(kept), left[:0]
    return pick(relative_masks(n, 1)), pick(kept[half:]), pick(kept[:half])


def product(left, at, rows, right, came=None, came_at=0):
    depth, columns = right.shape
    step = next(size for size in (512, 384, 256, 128) if columns % size == 0)
    arrays, specs = [left, right], [
        pl.BlockSpec((rows, depth), lambda j: (at, 0)),
        pl.BlockSpec((depth, step), lambda j: (0, j)),
    ]
    if came is not None:
        arrays.append(came)
        specs.append(pl.BlockSpec((rows, step), lambda j: (came_at, j)))

    def kernel(*refs):
        given = mm(refs[0][...], refs[1][...])
        refs[-1][...] = given if came is None else given + refs[2][...]

    return pl.pallas_call(
        kernel,
        grid=(columns // step,),
        in_specs=specs,
        out_specs=pl.BlockSpec((rows, step), lambda j: (0, j)),
        out_shape=shape(rows, columns),
        compiler_params=pltpu.CompilerParams(
            dimension_semantics=("arbitrary",), vmem_limit_bytes=VMEM
        ),
        cost_estimate=pl.CostEstimate(flops=1, bytes_accessed=1, transcendentals=0),
    )(*arrays)


class ScatteredProduct:
    def __init__(self, left, right, n, extra=None):
        self.n, self.stride, self.left, self.right, self.extra = n, 1, left, right, extra
        if n == 1:
            self.total = mm(left[1], right)
        else:
            self.send = mm(left[0], right)

    def start(self, *others):
        pairs = [(p, p ^ self.stride) for p in range(self.n)]
        if self.stride == 1 and self.extra is not None:
            self.extra = self.extra + lax.ppermute(self.extra, "dp", pairs)
        self.came = lax.ppermute(after(self.send, *others), "dp", pairs)

    def settle(self, *others):
        came = after(self.came, *others)
        if self.stride == 1:
            rows = self.left[2].shape[0]
            keep = mm(self.left[2], self.right) + came[:rows]
            send = mm(self.left[1], self.right) + came[rows:]
        else:
            size = self.keep.shape[0]
            rows = size // 2 if 2 * self.stride < self.n else 0
            if self.extra is not None:
                self.extra = self.extra + came[size:]
            keep, send = self.keep[:rows] + came[:rows], self.keep[rows:] + came[rows:size]
        self.stride *= 2
        if self.stride == self.n:
            self.total = send
            return
        if self.extra is not None:
            send = jnp.concatenate((send, self.extra), axis=0)
        self.keep, self.send = keep, send

    def finish(self):
        while self.stride < self.n:
            self.start()
            self.settle()
        return self.total


def after(values, *others):
    return lax.optimization_barrier((values,) + others)[0]


def tied(array, *waits):
    def nothing(*refs):
        pass

    anywhere = pl.BlockSpec(memory_space=pl.ANY)
    out = pl.pallas_call(
        nothing,
        in_specs=[anywhere] * (1 + len(waits)),
        out_specs=anywhere,
        out_shape=jax.ShapeDtypeStruct(array.shape, array.dtype),
        input_output_aliases={0: 0},
        cost_estimate=pl.CostEstimate(flops=1, bytes_accessed=1, transcendentals=0),
    )(array, *waits)
    return out


def swap_tensor(values, n):
    return lax.ppermute(values, "tensor", [(t, t ^ 1) for t in range(n)])


def body(
    block_input,
    norm_gain,
    z_weight,
    x_weight,
    bc_weight,
    dt_weight,
    x_conv,
    x_conv_bias,
    bc_conv,
    bc_conv_bias,
    dt_bias,
    a_log,
    d_skip,
    gated_gain,
    out_weight,
    out_cotangent,
):
    n_dp, n_tensor = lax.axis_size("dp"), lax.axis_size("tensor")
    rows, model = block_input.shape
    inner = x_weight.shape[1]
    head_count = dt_weight.shape[1]
    head_dim = inner // head_count
    states = bc_weight.shape[1] // 2
    taps = x_conv.shape[0]
    heads = 4
    width = heads * head_dim
    blocks = inner // width
    chunks = rows // SPAN
    per_seq = LEN // SPAN
    inner_total = inner * n_tensor
    me = lax.axis_index("dp").astype(jnp.int32).reshape(1)
    lanes = 128
    side_width = 2 * states + lanes

    def tripled(v):
        one = jnp.pad(v, ((0, 0), (0, GROUP - head_count)))
        return jnp.pad(jnp.concatenate((one, one, one), axis=1), ((0, 0), (0, lanes - 3 * GROUP)))

    dt_w = tripled(dt_weight)
    dt_b = tripled(dt_bias[None])
    a_l = tripled(a_log[None])
    skip = jnp.repeat(d_skip, head_dim)[None]
    packed = jnp.concatenate((x_conv, x_conv_bias[None], skip, gated_gain[None]), axis=0)
    packed = jnp.pad(packed, ((0, HALO - packed.shape[0] % HALO), (0, 0)))
    gain_in = norm_gain[None]
    bc_bias = bc_conv_bias[None]

    def whole(array):
        return (array, array.shape, lambda j: (0,) * array.ndim)

    def columns(array):
        return (array, (array.shape[0], width), lambda j: (0, j))

    shared = Named(
        norm_gain=whole(gain_in),
        x_w=columns(x_weight),
        z_w=columns(z_weight),
        bc_w=whole(bc_weight),
        dt_w=whole(dt_w),
        packed=columns(packed),
        bc_conv=whole(bc_conv),
        bc_conv_bias=whole(bc_bias),
        dt_bias=whole(dt_b),
        a_log=whole(a_l),
    )

    residual = block_input.astype(F32)
    inv_rms = lax.rsqrt(jnp.mean(residual * residual, axis=1, keepdims=True) + EPS)
    normed = (residual * inv_rms * gain_in).astype(BF16)
    side_pre = mm(normed, jnp.concatenate((bc_weight, dt_w), axis=1))
    bc_pre, dt_pre = side_pre[:, : 2 * states], side_pre[:, 2 * states :]
    x_pre = mm(normed, x_weight)
    z_pre = mm(normed, z_weight)

    kept = Named()
    shares = []
    shares_other = []
    states_at = []
    for i in range(chunks):
        first = i % per_seq == 0

        def at_rows(j, i=i):
            return (i, 0)

        def at_block(j, i=i):
            return (i, j)

        def at_turned(j, i=i):
            return (0, i)

        operands = Named()
        for name in ("packed", "bc_conv", "bc_conv_bias", "dt_bias", "a_log"):
            operands[name] = shared[name]
        operands.place = (me, None, None)
        operands.cot = (out_cotangent, (SPAN, model), at_rows)
        operands.out_w = (out_weight, (width, model), lambda j: (j, 0))
        operands.normed = (normed, (SPAN, model), at_rows)
        operands.bc_pre = (bc_pre, (SPAN, 2 * states), at_rows)
        operands.dt_pre = (dt_pre, (SPAN, lanes), at_rows)
        operands.x_pre = (x_pre, (SPAN, width), at_block)
        operands.z_pre = (z_pre, (SPAN, width), at_block)
        before = i * (SPAN // HALO) - 1
        if not first:
            operands.x_halo = (x_pre, (HALO, width), lambda j, b=before: (b, j))
            operands.bc_halo = (bc_pre, (HALO, 2 * states), lambda j, b=before: (b, 0))
            operands.state = columns(states_at[-1])
        outs = Named(
            u_out=(shape(SPAN, model), (SPAN, model), lambda j: (0, 0)),
            state_out=(shape(states, inner), (states, width), lambda j: (0, j)),
            sums=(shape(HALO, rows), (HALO, SPAN), lambda j, i=i: (0, i)),
            normed_t=(shape(model, rows, kind=BF16), (model, SPAN), at_turned),
            cot_t=(shape(model, rows, kind=BF16), (model, SPAN), at_turned),
            mixed=(shape(rows, inner), (SPAN, width), at_block),
        )
        waits = []
        scratch = Named(
            cb=((SPAN, 2 * states), BF16),
            bt=((2 * states, SPAN), BF16),
            scores=((SPAN, SPAN), F32),
            cum_t=((lanes, SPAN), F32),
            parts=((2 * SPAN, lanes), BF16),
            acc=((SPAN, width), F32),
        )
        given = run_kernel(
            functools.partial(fwd_kernel, first, heads, head_dim, blocks, n_dp),
            (blocks,),
            operands,
            outs,
            scratch,
            kept,
            waits,
        )
        shares.append(given.pop("u_out"))
        if i == 0:
            shares_other.append(swap_tensor(shares[-1], n_tensor))
        states_at.append(given.pop("state_out"))
        kept = given

    kept.x_pre, kept.z_pre, kept.bc_pre, kept.dt_pre = x_pre, z_pre, bc_pre, dt_pre
    sums = kept.sums
    sums_other = swap_tensor(sums, n_tensor)

    def sums_at(rows_of, at=lambda i: i):
        block = (HALO, rows_of)
        return {
            "sums": (sums, block, lambda i: (0, at(i))),
            "sums_other": (sums_other, block, lambda i: (0, at(i))),
        }

    operands = Named(sums_at(SPAN))
    operands.packed = (packed, packed.shape, lambda i: (0, 0))
    for name, array in dict(z_pre=kept.z_pre, mixed=kept.mixed).items():
        operands[name] = (array, (SPAN, inner), lambda i: (i, 0))
    operands.cot = (out_cotangent, (SPAN, model), lambda i: (i, 0))
    operands.out_w = (out_weight, out_weight.shape, lambda i: (0, 0))
    outs = Named(
        mg=(shape(rows, inner), (SPAN, inner), lambda i: (i, 0)),
        mixer_out=(shape(rows, inner, kind=BF16), (SPAN, inner), lambda i: (i, 0)),
        z_low=(shape(rows, inner, kind=BF16), (SPAN, inner), lambda i: (i, 0)),
    )
    gates = run_kernel(
        functools.partial(gate_kernel, inner_total, taps, width),
        (chunks,),
        operands,
        outs,
        Named(),
        Named(),
        shares_other[:1],
    )
    for share in shares[1:]:
        shares_other.append(swap_tensor(after(share, sums_other), n_tensor))

    def finished(body, given, out, ours, theirs, at):
        operands = Named(given)
        for name, array in dict(share=ours, share_other=theirs).items():
            operands[name] = (array, (part, model), lambda k: (k, 0))
        outs = Named(out=(shape(rows, model, kind=BF16), (part, model), lambda k: (at + k, 0)))
        carried = Named() if out is None else Named(out=out)
        return run_kernel(body, (ours.shape[0] // part,), operands, outs, Named(), carried).out

    def with_output(out, piece):
        at = piece * SPAN // part
        given = sums_at(part, lambda k: at + k)
        given["xin"] = (block_input, (part, model), lambda k: (at + k, 0))
        kernel = functools.partial(output_kernel, inner_total)
        return finished(kernel, given, out, shares[piece], shares_other[piece], at)

    part = SPAN // 2
    block_output = with_output(None, 0)

    out_product = product(kept.cot_t, 0, model, gates.mixer_out)
    z_low = tied(gates.z_low, *shares_other[1:2], out_product, *([block_output] if chunks > 1 else []))
    kept.z_low, kept.mg = z_low, gates.mg
    normed_left = arranged(kept.normed_t, n_dp)
    z_sum = ScatteredProduct(normed_left, z_low, n_dp)
    if n_dp > 1:
        z_sum.start()
        z_sum.settle()
    y_waits = {0: [out_product], 2: shares_other[2:3]}
    if n_dp > 2:
        z_sum.start()
        y_waits[0] = [out_product, z_sum.send]


    lows = Named()
    carry = Named()
    in_parts = [None] * chunks
    in_other = [None] * chunks
    queue = [sums_other] * 3
    for i in reversed(range(chunks)):
        first = i % per_seq == 0
        last_chunk = i % per_seq == per_seq - 1
        start = i == chunks - 1

        def at_rows(j, i=i):
            return (i, 0)

        def at_block(j, i=i):
            return (i, j)

        operands = Named(shared)
        operands.xin = (block_input, (SPAN, model), at_rows)
        for name in ("bc_pre", "dt_pre"):
            operands[name] = (kept[name], (SPAN, kept[name].shape[1]), at_rows)
        operands.x_w = (x_weight, (model, width), lambda j: (0, jnp.maximum(j - 1, 0)))
        operands.x_w_last = (x_weight, (model, width), lambda j: (0, blocks - 1))
        for name in ("x_pre", "z_pre", "mg", "mixed", "z_low"):
            operands[name] = (kept[name], (SPAN, width), at_block)
        operands.sums = (sums, (HALO, SPAN), lambda j, i=i: (0, i))
        operands.sums_other = (sums_other, (HALO, SPAN), lambda j, i=i: (0, i))
        before = i * (SPAN // HALO) - 1
        if not first:
            operands.x_halo = (kept.x_pre, (HALO, width), lambda j, b=before: (b, j))
            operands.bc_halo = (kept.bc_pre, (HALO, 2 * states), lambda j, b=before: (b, 0))
            operands.state = columns(states_at[i - 1])
        if not last_chunk:
            operands.d_state = columns(carry.d_state_out)
            operands.du_halo = columns(carry.du_halo_out)
            operands.du_bc_halo = whole(carry.du_bc_halo_out)
            operands.x_sums_in = columns(carry.x_sums)
            for name in ("head_sums", "bc_sums", "gain_sums"):
                operands[name + "_in"] = whole(carry[name])
        outs = Named(
            in_part=(shape(SPAN, model), (SPAN, model), lambda j: (0, 0)),
            du_halo_out=(shape(HALO, inner), (HALO, width), lambda j: (0, j)),
            du_bc_halo_out=(shape(HALO, 2 * states), (HALO, 2 * states), lambda j: (0, 0)),
            x_sums=(shape(HALO, inner), (HALO, width), lambda j: (0, j)),
            head_sums=(shape(HALO, lanes), (HALO, lanes), lambda j: (0, 0)),
            bc_sums=(shape(HALO, 2 * states), (HALO, 2 * states), lambda j: (0, 0)),
            gain_sums=(shape(HALO, model), (HALO, model), lambda j: (0, 0)),
            x_low=(shape(rows, inner, kind=BF16), (SPAN, width), at_block),
            side_low=(shape(rows, side_width, kind=BF16), (SPAN, side_width), at_rows),
        )
        waits = y_waits.get(chunks - 1 - i, [])
        if i == 0:
            waits = waits + queue[3:4]
        if not first:
            outs.d_state_out = (shape(states, inner), (states, width), lambda j: (0, j))
        scratch = Named(
            bc_slope=((SPAN, 2 * states), F32),
            bb=((SPAN, 2 * states), BF16),
            cb=((SPAN, 2 * states), BF16),
            ct=((2 * states, SPAN), BF16),
            scores=((SPAN, SPAN), F32),
            d_scores=((SPAN, SPAN), F32),
            dt=((SPAN, lanes), F32),
            cum_t=((lanes, SPAN), F32),
            parts=((2 * SPAN, lanes), BF16),
            db=((SPAN, states), F32),
            dc=((SPAN, states), F32),
            d_cum=((SPAN, lanes), F32),
            d_dt=((SPAN, lanes), F32),
            ng=((SPAN, model), F32),
            x_low_before=((SPAN, width), BF16),
            rows=((SPAN, lanes), F32),
        )
        given = run_kernel(
            functools.partial(bwd_kernel, first, last_chunk, heads, head_dim, inner_total),
            (blocks,),
            operands,
            outs,
            scratch,
            lows,
            waits,
        )
        lows = Named(x_low=given.x_low, side_low=given.side_low)
        in_parts[i] = given.in_part
        queue.append(swap_tensor(in_parts[i], n_tensor))
        in_other[i] = queue[-1]
        if last_chunk and not start:
            for name in ("x_sums", "head_sums", "bc_sums", "gain_sums"):
                given[name] = given[name] + carry[name]
        carry = given

    cut = inner // 2
    z_wait = []
    if n_dp > 4:
        z_sum.settle(carry.head_sums)
        z_sum.start()
        z_wait = [z_sum.send]
    x_low = tied(lows.x_low, *queue[4:5], *z_wait)
    small = jnp.concatenate(
        (
            carry.x_sums[: taps + 3].reshape(-1),
            carry.head_sums[:2, :head_count].reshape(-1),
            carry.gain_sums[0],
            carry.bc_sums[: taps + 1].reshape(-1),
        )
    )
    near_width = cut + side_width
    extra = jnp.pad(small, (0, -small.shape[0] % (16 * near_width))).reshape(-1, near_width)
    near_low = jnp.concatenate((x_low[:, :cut], lows.side_low), axis=1)
    near = ScatteredProduct(normed_left, near_low, n_dp, extra)
    far = ScatteredProduct(normed_left, x_low[:, cut:], n_dp)
    out_part = lax.psum_scatter(out_product, "dp", scatter_dimension=0, tiled=True)
    order = []
    for i in range(1, len(shares)):
        block_output = with_output(block_output, i)

    def with_grad(out, i):
        given = dict(cot=(out_cotangent, (part, model), lambda k: (i * 2 + k, 0)))
        return finished(grad_kernel, given, out, in_parts[i], in_other[i], i * 2)

    input_grads = []
    for i in reversed(range(2, chunks)):
        input_grads.append(with_grad(input_grads[-1] if input_grads else None, i))
    input_grad = input_grads[-1] if input_grads else None
    starts = {(True, 2): [out_part]}
    starts[False, 4] = input_grads[-1:] + queue[5:6]
    if n_dp > 4:
        z_sum.settle(x_low)
        z_sum.start()
        starts[False, 2] = [z_sum.send]

    def step(sum_of):
        if sum_of.stride < n_dp:
            sum_of.settle(*order)
            done = sum_of.stride == n_dp
            order[:] = [sum_of.total if done else sum_of.send]
            if not done:
                sum_of.start(*starts.get((sum_of is near, sum_of.stride), []))

    for one in (near, far):
        if n_dp > 1:
            one.start()
    for one in (near, far, near):
        step(one)
    while z_sum.stride < n_dp:
        step(z_sum)
    starts[False, 4].append(z_sum.total)
    for one in (far, near) * 8:
        step(one)
    z_weight_grad = z_sum.total
    near_part, far = near.total, far.total
    small = near.extra.reshape(-1)
    side_part = near_part[:, cut:]
    x_weight_grad = jnp.concatenate((near_part[:, :cut], far), axis=1)
    bc_part = side_part[:, : 2 * states]
    dt_weight_grad = side_part[:, 2 * states : 2 * states + head_count]

    bc_part = bc_part.reshape(n_tensor, -1, 2 * states)
    mine = lax.axis_index("tensor")
    theirs = lax.dynamic_index_in_dim(bc_part, 1 - mine, 0, keepdims=False)
    shared_at = (taps + 3) * inner + 2 * head_count
    shared_sums = small[shared_at : shared_at + model + (taps + 1) * 2 * states]
    shared_sums = jnp.pad(shared_sums, (0, -shared_sums.shape[0] % (HALO * 2 * states)))
    shared_sums = shared_sums.reshape(-1, 2 * states)
    ours = lax.dynamic_index_in_dim(bc_part, mine, 0, keepdims=False)
    mixed_rows = jnp.concatenate((theirs, shared_sums), axis=0)
    came = swap_tensor(after(mixed_rows, block_output), n_tensor)
    bc_weight_grad = ours + came[: ours.shape[0]]
    shared_sums = (shared_sums + came[ours.shape[0] :]).reshape(-1)

    x_end = (taps + 3) * inner
    x_sums = small[:x_end].reshape(taps + 3, inner)
    gated_gain_grad = x_sums[0]
    d_skip_grad = x_sums[1].reshape(head_count, head_dim).sum(axis=1)
    x_conv_grad = x_sums[2 : taps + 2]
    x_conv_bias_grad = x_sums[taps + 2]
    dt_bias_grad = small[x_end : x_end + head_count]
    a_log_grad = small[x_end + head_count : x_end + 2 * head_count]
    gain_total = shared_sums[:model]
    bc_total = shared_sums[model : model + (taps + 1) * 2 * states].reshape(taps + 1, 2 * states)
    place = lax.axis_index("dp") * n_tensor + lax.axis_index("tensor")
    places = n_dp * n_tensor

    def own(values, axis):
        size = values.shape[axis] // places
        return lax.dynamic_slice_in_dim(values, place * size, size, axis)

    norm_gain_grad = own(gain_total, 0)
    bc_conv_grad = own(bc_total[:taps], 1)
    bc_conv_bias_grad = own(bc_total[taps], 0)

    out_weight_grad = out_part.T

    if chunks > 1:
        input_grad = with_grad(input_grad, 1)
    in_other[0] = after(in_other[0], far)
    input_grad = with_grad(input_grad, 0)
    return (
        block_output,
        input_grad,
        norm_gain_grad,
        z_weight_grad,
        x_weight_grad,
        bc_weight_grad,
        dt_weight_grad,
        x_conv_grad,
        x_conv_bias_grad,
        bc_conv_grad,
        bc_conv_bias_grad,
        dt_bias_grad,
        a_log_grad,
        d_skip_grad,
        gated_gain_grad,
        out_weight_grad,
    )


def solution(mesh):
    in_specs = (
        P("dp", None),
        P(),
        P(None, "tensor"),
        P(None, "tensor"),
        P(),
        P(None, "tensor"),
        P(None, "tensor"),
        P("tensor"),
        P(),
        P(),
        P("tensor"),
        P("tensor"),
        P("tensor"),
        P("tensor"),
        P("tensor", None),
        P("dp", None),
    )
    out_specs = (
        P("dp", None),
        P("dp", None),
        P(("dp", "tensor")),
        P("dp", "tensor"),
        P("dp", "tensor"),
        P(("dp", "tensor"), None),
        P("dp", "tensor"),
        P(None, "tensor"),
        P("tensor"),
        P(None, ("dp", "tensor")),
        P(("dp", "tensor")),
        P("tensor"),
        P("tensor"),
        P("tensor"),
        P("tensor"),
        P("tensor", "dp"),
    )
    return jax.shard_map(body, mesh=mesh, in_specs=in_specs, out_specs=out_specs, check_vma=False)
```

profile of v0, /device:TPU:14, one launch (start us, length us, event | category | flops | bytes accessed | tf_op | source)
XLA Modules:
  0.0 417.6 jit_solution(16571541083266276517)
XLA Ops:
  7.3 2.7 fusion
  16.9 10.5 %fusion.38.refs_12_.refs_3_.refs_15_ = f32[1024,1536]{1,0:T(8,128)} fusion(bf16[1024,1536]{1,0:T(8,128)(2,1)} %copy-done.3, bf16[1536,1536]{1,0:T(8,128)(2,1)} %refs_2_.15), kind=kOutput, calls=%fused_computation.84 | convolution fusion | flops 4831838208 | bytes 14155776 | tf_op jit(solution)/shard_map/dot_general | solution.py:29
  27.4 7.0 %fusion.37.refs_11_.refs_13_.refs_14_.refs_21_ = f32[1024,1536]{1,0:T(8,128)} fusion(bf16[1024,1536]{1,0:T(8,128)(2,1)S(1)} %copy-done.4, bf16[1536,1536]{1,0:T(8,128)(2,1)S(1)} %bitcast.23), kind=kOutput, calls=%fused_computation.83 | convolution fusion | flops 4831838208 | bytes 14155776 | tf_op jit(solution)/shard_map/dot_general | solution.py:29
  35.6 12.7 %shard_map.279 = (f32[256,1536]{1,0:T(8,128)}, f32[128,1536]{1,0:T(8,128)}, f32[8,1024]{1,0:T(8,128)}, bf16[1536,1024]{1,0:T(8,128)(2,1)}, bf16[1536,1024]{1,0:T(8,128)(2,1)}, /*index=5*/f32[1024,1536]{1,0:T(8,128)}) custom-call(f32[8,1536]{1,0:T(8,128)} %select_maximum_fusion.refs_0_.refs_2_.refs_5_, f32[4,256]{1,0:T(4,128)} %refs_6_.17, ...), custom_call_target="tpu_custom_call" | custom-call | flops 1 | bytes 1 | tf_op jit(solution)/shard_map/pallas_call | solution.py:532
  48.9 13.7 %shard_map.280 = (f32[256,1536]{1,0:T(8,128)}, f32[128,1536]{1,0:T(8,128)}, f32[8,1024]{1,0:T(8,128)}, bf16[1536,1024]{1,0:T(8,128)(2,1)}, bf16[1536,1024]{1,0:T(8,128)(2,1)}, /*index=5*/f32[1024,1536]{1,0:T(8,128)}) custom-call(f32[8,1536]{1,0:T(8,128)} %select_maximum_fusion.refs_0_.ref, ...), custom_call_target="tpu_custom_call", output_to_operand_aliasing={{2}: (16, {}), {3}: (17, {}), {4}: (18, {}), {5}: (19, {})} | custom-call | flops 1 | bytes 1 | tf_op jit(solution)/shard_map/pallas_call | solution.py:532
  62.6 13.7 %shard_map.281 = (f32[256,1536]{1,0:T(8,128)}, f32[128,1536]{1,0:T(8,128)}, f32[8,1024]{1,0:T(8,128)}, bf16[1536,1024]{1,0:T(8,128)(2,1)}, bf16[1536,1024]{1,0:T(8,128)(2,1)}, /*index=5*/f32[1024,1536]{1,0:T(8,128)}) custom-call(f32[8,1536]{1,0:T(8,128)} %select_maximum_fusion.refs_0_.ref, ...), custom_call_target="tpu_custom_call", output_to_operand_aliasing={{2}: (16, {}), {3}: (17, {}), {4}: (18, {}), {5}: (19, {})} | custom-call | flops 1 | bytes 1 | tf_op jit(solution)/shard_map/pallas_call | solution.py:532
  76.3 13.7 %shard_map.282 = (f32[256,1536]{1,0:T(8,128)}, f32[128,1536]{1,0:T(8,128)}, f32[8,1024]{1,0:T(8,128)}, bf16[1536,1024]{1,0:T(8,128)(2,1)}, bf16[1536,1024]{1,0:T(8,128)(2,1)}, /*index=5*/f32[1024,1536]{1,0:T(8,128)}) custom-call(f32[8,1536]{1,0:T(8,128)} %select_maximum_fusion.refs_0_.ref, ...), custom_call_target="tpu_custom_call", output_to_operand_aliasing={{2}: (16, {}), {3}: (17, {}), {4}: (18, {}), {5}: (19, {})} | custom-call | flops 1 | bytes 1 | tf_op jit(solution)/shard_map/pallas_call | solution.py:532
  91.5 2.6 collective-permute-done.refs_1_.refs_20_
  96.8 15.6 %shard_map.287 = (f32[1024,1536]{1,0:T(8,128)}, bf16[1024,1536]{1,0:T(8,128)(2,1)}, bf16[1024,1536]{1,0:T(8,128)(2,1)}) custom-call(f32[8,1024]{1,0:T(8,128)} %get-tuple-element.112.refs_0_.refs_19_, f32[8,1024]{1,0:T(8,128)} %copy-done.19, f32[8,1536]{1,0:T(8,128)} %select_maximum_fusion.refs_0_.refs_2_.refs_5_, ...), custom_call_target="tpu_custom_call" | custom-call | flops 1 | bytes 1 | tf_op jit(solution)/shard_map/pallas_call | solution.py:532
  112.4 9.6 %shard_map.288.refs_2_.refs_24_ = f32[1536,1536]{1,0:T(8,128)} custom-call(bf16[1536,1024]{1,0:T(8,128)(2,1)} %get-tuple-element.123.refs_0_, bf16[1024,1536]{1,0:T(8,128)(2,1)} %get-tuple-element.124.refs_1_), custom_call_target="tpu_custom_call" | custom-call | flops 1 | bytes 1 | tf_op jit(solution)/shard_map/pallas_call | solution.py:595
  122.1 3.1 shard_map.283.refs_5_.refs_3_
  125.2 3.9 collective-permute-done.3.refs_4_.refs_1_
  130.3 2.3 copy-done.6
  132.6 5.0 %fusion.10 = f32[768,1536]{1,0:T(8,128)S(1)} fusion(bf16[1024,1536]{1,0:T(8,128)(2,1)} %shard_map.289.refs_18_, bf16[1536,1024]{1,0:T(8,128)(2,1)S(1)} %copy-done.6), kind=kOutput, calls=%fused_computation.20 | convolution fusion | flops 2415919104 | bytes 9437184 | tf_op jit(solution)/shard_map/dot_general | solution.py:29
  137.6 9.5 %collective-permute-done.5 = f32[768,1536]{1,0:T(8,128)S(1)} collective-permute-done((f32[768,1536]{1,0:T(8,128)S(1)}, f32[768,1536]{1,0:T(8,128)S(1)}, u32[]{:S(2)}, u32[]{:S(2)}) %collective-permute-start.5) | collective-permute-done | bytes 4718624 | tf_op jit(solution)/shard_map/ppermute | solution.py:620
  147.1 2.9 convolution_add_fusion.3.refs_25_
  152.5 19.8 %shard_map.290 = (f32[256,1536]{1,0:T(8,128)}, f32[8,1536]{1,0:T(8,128)}, f32[8,256]{1,0:T(8,128)}, f32[8,1536]{1,0:T(8,128)}, f32[8,128]{1,0:T(8,128)}, /*index...) custom-call(f32[1,1536]{1,0:T(1,128)} %broadcast_in_dim.28.refs_0_, ...), custom_call_target="tpu_custom_call" | custom-call | flops 1 | bytes 1 | tf_op jit(solution)/shard_map/pallas_call | solution.py:532
  172.9 20.7 %shard_map.291 = (f32[256,1536]{1,0:T(8,128)}, f32[8,1536]{1,0:T(8,128)}, f32[8,256]{1,0:T(8,128)}, f32[8,1536]{1,0:T(8,128)}, f32[8,128]{1,0:T(8,128)}, /*index...) custom-call(f32[1,1536]{1,0:T(1,128)} %broadcast_in_dim.28.refs_0_, ...), custom_call_target="tpu_custom_call", output_to_operand_aliasing={{7}: (31, {}), {8}: (32, {})} | custom-call | flops 1 | bytes 1 | tf_op jit(solution)/shard_map/pallas_call | solution.py:532
  196.5 20.8 %shard_map.292 = (f32[256,1536]{1,0:T(8,128)}, f32[8,1536]{1,0:T(8,128)}, f32[8,256]{1,0:T(8,128)}, f32[8,1536]{1,0:T(8,128)}, f32[8,128]{1,0:T(8,128)}, /*index...) custom-call(f32[1,1536]{1,0:T(1,128)} %broadcast_in_dim.28.refs_0_, ...), custom_call_target="tpu_custom_call", output_to_operand_aliasing={{7}: (31, {}), {8}: (32, {})} | custom-call | flops 1 | bytes 1 | tf_op jit(solution)/shard_map/pallas_call | solution.py:532
  217.2 4.4 %convolution_add_fusion.2 = f32[384,1536]{1,0:T(8,128)} fusion(bf16[1024,1536]{1,0:T(8,128)(2,1)S(1)} %copy-done.2, f32[768,1536]{1,0:T(8,128)} %copy-done.33, bf16[1536,1024]{1,0:T(8,128)(2,1)S(1)} %copy-done.6), kind=kOutput, calls=%fused_computation.7 | convolution fusion | flops 1208549376 | bytes 8650752 | tf_op jit(solution)/shard_map/dot_general | solution.py:29
  222.8 21.5 %shard_map.293 = (f32[256,1536]{1,0:T(8,128)}, f32[8,1536]{1,0:T(8,128)}, f32[8,256]{1,0:T(8,128)}, f32[8,1536]{1,0:T(8,128)}, f32[8,128]{1,0:T(8,128)}, /*index...) custom-call(f32[1,1536]{1,0:T(1,128)} %broadcast_in_dim.28.refs_0_, ...), custom_call_target="tpu_custom_call", output_to_operand_aliasing={{7}: (28, {}), {8}: (29, {})} | custom-call | flops 1 | bytes 1 | tf_op jit(solution)/shard_map/pallas_call | solution.py:532
  244.3 3.4 slice_add_fusion
  247.7 6.4 %collective-permute-done.8.refs_1_.refs_2_ = f32[256,1536]{1,0:T(8,128)} collective-permute-done((f32[256,1536]{1,0:T(8,128)}, f32[256,1536]{1,0:T(8,128)}, u32[]{:S(2)}, u32[]{:S(2)}) %collective-permute-start.8) | collective-permute-done | bytes 1572896 | tf_op jit(solution)/shard_map/ppermute | solution.py:670
  256.5 5.2 %fusion.7 = f32[768,1152]{1,0:T(8,128)} fusion(bf16[1536,1024]{1,0:T(8,128)(2,1)S(1)} %copy-done.7, bf16[1024,384]{1,0:T(8,128)(2,1)} %get-tuple-element.159, bf16[1024,768]{1,0:T(8,128)(2,1)S(1)} %slice.277), kind=kOutput, calls=%fused_computation.17 | convolution fusion | flops 1816657920 | bytes 7471104 | tf_op jit(solution)/shard_map/dot_general | solution.py:29
  261.8 2.9 fusion.4
  266.9 4.5 %collective-permute-done.12 = f32[16,1152]{1,0:T(8,128)S(1)} collective-permute-done((f32[16,1152]{1,0:T(8,128)S(1)}, f32[16,1152]{1,0:T(8,128)S(1)}, u32[]{:S(2)}, u32[]{:S(2)}) %collective-permute-start.12) | collective-permute-done | bytes 73760 | tf_op jit(solution)/shard_map/ppermute | solution.py:619
  272.1 3.6 convolution_add_fusion.1
  280.2 2.9 shard_map.295.refs_3_
  283.4 3.2 shard_map.296.refs_3_
  286.6 13.2 %collective-permute-done.13 = f32[192,1536]{1,0:T(8,128)} collective-permute-done((f32[192,1536]{1,0:T(8,128)}, f32[192,1536]{1,0:T(8,128)}, u32[]{:S(2)}, u32[]{:S(2)}) %collective-permute-start.13) | collective-permute-done | bytes 1179680 | tf_op jit(solution)/shard_map/ppermute | solution.py:620
  301.3 2.9 collective-permute-start.15
  304.2 2.0 convolution_add_fusion.4
  307.6 2.7 convolution_add_fusion
  310.3 10.2 %collective-permute-done.16 = f32[400,1152]{1,0:T(8,128)} collective-permute-done((f32[400,1152]{1,0:T(8,128)}, f32[400,1152]{1,0:T(8,128)}, u32[]{:S(2)}, u32[]{:S(2)}) %collective-permute-start.16) | collective-permute-done | bytes 1843232 | tf_op jit(solution)/shard_map/ppermute | solution.py:620
  324.7 2.0 convolution_add_fusion.5
  326.7 2.2 collective-permute-done.15
  328.9 2.0 fusion.25
  330.9 13.6 %collective-permute-done.14 = f32[384,768]{1,0:T(8,128)S(1)} collective-permute-done((f32[384,768]{1,0:T(8,128)S(1)}, f32[384,768]{1,0:T(8,128)S(1)}, u32[]{:S(2)}, u32[]{:S(2)}) %collective-permute-start.14) | collective-permute-done | bytes 1179680 | tf_op jit(solution)/shard_map/ppermute | solution.py:620
  345.5 3.0 collective-permute-done.17.refs_2_
  351.3 2.6 collective-permute-start.21
  353.9 3.1 shard_map.284.refs_5_
  357.0 3.1 shard_map.285.refs_5_
  360.2 3.2 shard_map.286
  364.7 2.9 shard_map.297.refs_3_
  367.6 4.6 %collective-permute-done.18 = f32[192,768]{1,0:T(8,128)} collective-permute-done((f32[192,768]{1,0:T(8,128)}, f32[192,768]{1,0:T(8,128)}, u32[]{:S(2)}, u32[]{:S(2)}) %collective-permute-start.18) | collective-permute-done | bytes 589856 | tf_op jit(solution)/shard_map/ppermute | solution.py:620
  374.0 9.7 %collective-permute-done.21 = f32[112,1152]{1,0:T(8,128)} collective-permute-done((f32[112,1152]{1,0:T(8,128)}, f32[112,1152]{1,0:T(8,128)}, u32[]{:S(2)}, u32[]{:S(2)}) %collective-permute-start.21) | collective-permute-done | bytes 516128 | tf_op jit(solution)/shard_map/ppermute | solution.py:620
  391.4 8.2 %collective-permute-done.7.refs_2_ = f32[256,1536]{1,0:T(8,128)} collective-permute-done((f32[256,1536]{1,0:T(8,128)S(1)}, f32[256,1536]{1,0:T(8,128)}, u32[]{:S(2)}, u32[]{:S(2)}) %collective-permute-start.7) | collective-permute-done | bytes 1572896 | tf_op jit(solution)/shard_map/ppermute | solution.py:670
  403.8 2.9 shard_map.298
  (178 shorter events, 60.7 us)
Async XLA Ops:
  7.2 4.4 %copy-start = (bf16[1024,1536]{1,0:T(8,128)(2,1)S(1)}, bf16[1024,1536]{1,0:T(8,128)(2,1)}, u32[]{:S(2)}) copy-start(bf16[1024,1536]{1,0:T(8,128)(2,1)} %refs_10_.7) | copy-start | bytes 9437188
  7.2 4.4 %copy-start.27 = (f32[1536]{0:T(1024)S(1)}, f32[1536]{0:T(1024)}, u32[]{:S(2)}) copy-start(f32[1536]{0:T(1024)} %param.17) | copy-start | bytes 18436
  7.2 269.8 %reduce-scatter.2.cloned.1.call-start = ((), (), s32[]{:S(2)}) async-start(), calls=%async_computation.1 | async-start | bytes 10027008 | tf_op jit(solution)/shard_map/reduce_scatter | solution.py:988
  15.6 11.8 %slice-start = ((s8[4718592]{0:T(1024)(128)(4,1)}), s8[524288]{0:T(1024)(128)(4,1)S(1)}, s32[]{:S(2)}) async-start(s8[4718592]{0:T(1024)(128)(4,1)} %bitcast.22), calls=%async_computation.2 | async-start | bytes 1048576
  16.9 10.5 %slice-start.1 = ((s8[4718592]{0:T(1024)(128)(4,1)}), s8[4194304]{0:T(1024)(128)(4,1)S(1)}, s32[]{:S(2)}) async-start(s8[4718592]{0:T(1024)(128)(4,1)} %bitcast.22), calls=%async_computation.3 | async-start | bytes 8388608
  16.9 10.5 %copy-start.4 = (bf16[1024,1536]{1,0:T(8,128)(2,1)S(1)}, bf16[1024,1536]{1,0:T(8,128)(2,1)}, u32[]{:S(2)}) copy-start(bf16[1024,1536]{1,0:T(8,128)(2,1)} %copy-done.3) | copy-start | bytes 9437188
  27.4 7.6 %copy-start.28 = (f32[4,1536]{1,0:T(4,128)S(1)}, f32[4,1536]{1,0:T(4,128)}, u32[]{:S(2)}) copy-start(f32[4,1536]{1,0:T(4,128)} %param.22) | copy-start | bytes 73732
  48.4 47.3 %collective-permute-start.4 = (f32[256,1536]{1,0:T(8,128)}, f32[256,1536]{1,0:T(8,128)S(1)}, u32[]{:S(2)}, u32[]{:S(2)}) collective-permute-start(f32[256,1536]{1,0:T(8,128)} %get-tuple-element.119.refs_3_), channel_id=1, source_target_pairs={{0,1},{1,0},{2,3},{3,2},{4,5},{5,4},{6,7},{7,6},{8,9},{9,8},{10,11... | collective-permute-start | bytes 4718600 | tf_op jit(solution)/shard_map/ppermute | solution.py:670
  90.0 4.2 %collective-permute-start = (f32[8,1024]{1,0:T(8,128)}, f32[8,1024]{1,0:T(8,128)S(1)}, u32[]{:S(2)}, u32[]{:S(2)}) collective-permute-start(f32[8,1024]{1,0:T(8,128)} %get-tuple-element.112.refs_0_.refs_19_), channel_id=1, source_target_pairs={{0,1},{1,0},{2,3},{3,2},{4,5},{5,4},{6,7},{7,6},{8,9},{9,8},{10,11... | collective-permute-start | bytes 98312 | tf_op jit(solution)/shard_map/ppermute | solution.py:670
  94.2 34.9 %collective-permute-start.3 = (f32[256,1536]{1,0:T(8,128)}, f32[256,1536]{1,0:T(8,128)S(1)}, u32[]{:S(2)}, u32[]{:S(2)}) collective-permute-start(f32[256,1536]{1,0:T(8,128)} %get-tuple-element.118.refs_3_), channel_id=1, source_target_pairs={{0,1},{1,0},{2,3},{3,2},{4,5},{5,4},{6,7},{7,6},{8,9},{9,8},{10,11... | collective-permute-start | bytes 4718600 | tf_op jit(solution)/shard_map/ppermute | solution.py:670
  130.3 2.3 copy-start.6
  132.6 14.6 %copy-start.1 = (bf16[1024,1536]{1,0:T(8,128)(2,1)S(1)}, bf16[1024,1536]{1,0:T(8,128)(2,1)}, u32[]{:S(2)}) copy-start(bf16[1024,1536]{1,0:T(8,128)(2,1)} %shard_map.289.refs_18_) | copy-start | bytes 9437188
  137.5 12.8 %copy-start.21 = (f32[256,1536]{1,0:T(8,128)S(1)}, f32[256,1536]{1,0:T(8,128)}, u32[]{:S(2)}) copy-start(f32[256,1536]{1,0:T(8,128)} %get-tuple-element.116.refs_3_) | copy-start | bytes 4718596
  137.5 9.6 %collective-permute-start.5 = (f32[768,1536]{1,0:T(8,128)S(1)}, f32[768,1536]{1,0:T(8,128)S(1)}, u32[]{:S(2)}, u32[]{:S(2)}) collective-permute-start(f32[768,1536]{1,0:T(8,128)S(1)} %fusion.10), channel_id=1, source_target_pairs={{0,2},{2,0},{4,6},{6,4},{8,10},{10,8},{12,14},{14,12},{16,18},{18,... | collective-permute-start | bytes 14155784 | tf_op jit(solution)/shard_map/ppermute | solution.py:620
  147.1 3.1 copy-start.33
  150.3 94.0 %collective-permute-start.9 = (f32[384,1536]{1,0:T(8,128)}, f32[384,1536]{1,0:T(8,128)}, u32[]{:S(2)}, u32[]{:S(2)}) collective-permute-start(f32[384,1536]{1,0:T(8,128)} %convolution_add_fusion.3.refs_25_), channel_id=1, source_target_pairs={{0,4},{2,6},{4,0},{6,2},{8,12},{10,14},{12,8},{14,10},{16,20},{18,... | collective-permute-start | bytes 7077896 | tf_op jit(solution)/shard_map/ppermute | solution.py:620
  150.3 45.0 %collective-permute-start.2 = (f32[256,1536]{1,0:T(8,128)S(1)}, f32[256,1536]{1,0:T(8,128)S(1)}, u32[]{:S(2)}, u32[]{:S(2)}) collective-permute-start(f32[256,1536]{1,0:T(8,128)S(1)} %copy-done.21), channel_id=1, source_target_pairs={{0,1},{1,0},{2,3},{3,2},{4,5},{5,4},{6,7},{7,6},{8,9},{9,8},{10,11... | collective-permute-start | bytes 4718600 | tf_op jit(solution)/shard_map/ppermute | solution.py:670
  172.4 49.3 %collective-permute-start.6 = (f32[256,1536]{1,0:T(8,128)}, f32[256,1536]{1,0:T(8,128)S(1)}, u32[]{:S(2)}, u32[]{:S(2)}) collective-permute-start(f32[256,1536]{1,0:T(8,128)} %get-tuple-element.153.refs_1_), channel_id=1, source_target_pairs={{0,1},{1,0},{2,3},{3,2},{4,5},{5,4},{6,7},{7,6},{8,9},{9,8},{10,11... | collective-permute-start | bytes 4718600 | tf_op jit(solution)/shard_map/ppermute | solution.py:670
  193.7 60.4 %collective-permute-start.8 = (f32[256,1536]{1,0:T(8,128)}, f32[256,1536]{1,0:T(8,128)}, u32[]{:S(2)}, u32[]{:S(2)}) collective-permute-start(f32[256,1536]{1,0:T(8,128)} %get-tuple-element.156.refs_1_), channel_id=1, source_target_pairs={{0,1},{1,0},{2,3},{3,2},{4,5},{5,4},{6,7},{7,6},{8,9},{9,8},{10,11... | collective-permute-start | bytes 4718600 | tf_op jit(solution)/shard_map/ppermute | solution.py:670
  196.5 20.8 %copy-start.2 = (bf16[1024,1536]{1,0:T(8,128)(2,1)S(1)}, bf16[1024,1536]{1,0:T(8,128)(2,1)}, u32[]{:S(2)}) copy-start(bf16[1024,1536]{1,0:T(8,128)(2,1)} %shard_map.289.refs_18_) | copy-start | bytes 9437188
  222.8 21.5 %copy-start.20 = (f32[384,1536]{1,0:T(8,128)S(1)}, f32[384,1536]{1,0:T(8,128)}, u32[]{:S(2)}) copy-start(f32[384,1536]{1,0:T(8,128)} %convolution_add_fusion.2) | copy-start | bytes 7077892
  254.1 2.4 copy-start.7
  255.8 5.9 %copy-start.23 = (bf16[1024,768]{1,0:T(8,128)(2,1)}, bf16[1024,768]{1,0:T(8,128)(2,1)S(1)}, u32[]{:S(2)}) copy-start(bf16[1024,768]{1,0:T(8,128)(2,1)S(1)} %slice.277) | copy-start | bytes 4718596
  256.5 5.2 %copy-start.5 = (bf16[1024,1536]{1,0:T(8,128)(2,1)S(1)}, bf16[1024,1536]{1,0:T(8,128)(2,1)}, u32[]{:S(2)}) copy-start(bf16[1024,1536]{1,0:T(8,128)(2,1)} %shard_map.294) | copy-start | bytes 9437188
  261.7 4.1 copy-start.26
  261.7 4.2 copy-start.31
  261.7 10.3 %collective-permute-start.11 = (f32[768,1152]{1,0:T(8,128)}, f32[768,1152]{1,0:T(8,128)}, u32[]{:S(2)}, u32[]{:S(2)}) collective-permute-start(f32[768,1152]{1,0:T(8,128)} %fusion.7), channel_id=1, source_target_pairs={{0,2},{2,0},{4,6},{6,4},{8,10},{10,8},{12,14},{14,12},{16,18},{18,... | collective-permute-start | bytes 10616840 | tf_op jit(solution)/shard_map/ppermute | solution.py:620
  264.6 39.6 %collective-permute-start.10 = (f32[768,768]{1,0:T(8,128)}, f32[768,768]{1,0:T(8,128)}, u32[]{:S(2)}, u32[]{:S(2)}) collective-permute-start(f32[768,768]{1,0:T(8,128)} %fusion.4), channel_id=1, source_target_pairs={{0,2},{2,0},{4,6},{6,4},{8,10},{10,8},{12,14},{14,12},{16,18},{18,... | collective-permute-start | bytes 7077896 | tf_op jit(solution)/shard_map/ppermute | solution.py:620
  266.8 4.6 %collective-permute-start.12 = (f32[16,1152]{1,0:T(8,128)S(1)}, f32[16,1152]{1,0:T(8,128)S(1)}, u32[]{:S(2)}, u32[]{:S(2)}) collective-permute-start(f32[16,1152]{1,0:T(8,128)S(1)} %reshape.91), channel_id=1, source_target_pairs={{0,2},{2,0},{4,6},{6,4},{8,10},{10,8},{12,14},{14,12},{16,18},{18,... | collective-permute-start | bytes 221192 | tf_op jit(solution)/shard_map/ppermute | solution.py:619
  271.4 28.4 %collective-permute-start.13 = (f32[192,1536]{1,0:T(8,128)}, f32[192,1536]{1,0:T(8,128)}, u32[]{:S(2)}, u32[]{:S(2)}) collective-permute-start(f32[192,1536]{1,0:T(8,128)} %get-tuple-element.211.refs_2_), channel_id=1, source_target_pairs={{0,8},{2,10},{4,12},{6,14},{8,0},{10,2},{12,4},{14,6},{16,24},{18,... | collective-permute-start | bytes 3538952 | tf_op jit(solution)/shard_map/ppermute | solution.py:620
  277.0 43.4 %collective-permute-start.16 = (f32[400,1152]{1,0:T(8,128)}, f32[400,1152]{1,0:T(8,128)}, u32[]{:S(2)}, u32[]{:S(2)}) collective-permute-start(f32[400,1152]{1,0:T(8,128)} %pad_maximum_fusion.1), channel_id=1, source_target_pairs={{0,4},{2,6},{4,0},{6,2},{8,12},{10,14},{12,8},{14,10},{16,20},{18,... | collective-permute-start | bytes 5529608 | tf_op jit(solution)/shard_map/ppermute | solution.py:620
  278.5 81.7 %collective-permute-start.1 = (f32[256,1536]{1,0:T(8,128)}, f32[256,1536]{1,0:T(8,128)}, u32[]{:S(2)}, u32[]{:S(2)}) collective-permute-start(f32[256,1536]{1,0:T(8,128)} %get-tuple-element.114.refs_3_), channel_id=1, source_target_pairs={{0,1},{1,0},{2,3},{3,2},{4,5},{5,4},{6,7},{7,6},{8,9},{9,8},{10,11... | collective-permute-start | bytes 4718600 | tf_op jit(solution)/shard_map/ppermute | solution.py:670
  283.1 21.1 %copy-start.8 = (bf16[1536,1024]{1,0:T(8,128)(2,1)S(1)}, bf16[1536,1024]{1,0:T(8,128)(2,1)}, u32[]{:S(2)}) copy-start(bf16[1536,1024]{1,0:T(8,128)(2,1)} %get-tuple-element.125) | copy-start | bytes 9437188
  283.1 65.3 %collective-permute-start.17 = (f32[256,1536]{1,0:T(8,128)}, f32[256,1536]{1,0:T(8,128)}, u32[]{:S(2)}, u32[]{:S(2)}) collective-permute-start(f32[256,1536]{1,0:T(8,128)} %get-tuple-element.170.refs_1_), channel_id=1, source_target_pairs={{0,1},{1,0},{2,3},{3,2},{4,5},{5,4},{6,7},{7,6},{8,9},{9,8},{10,11... | collective-permute-start | bytes 4718600 | tf_op jit(solution)/shard_map/ppermute | solution.py:670
  299.8 7.7 %copy-start.11 = (bf16[1024,384]{1,0:T(8,128)(2,1)S(1)}, bf16[1024,384]{1,0:T(8,128)(2,1)}, u32[]{:S(2)}) copy-start(bf16[1024,384]{1,0:T(8,128)(2,1)} %get-tuple-element.159) | copy-start | bytes 2359300
  299.8 7.7 %copy-start.24 = (bf16[1024,768]{1,0:T(8,128)(2,1)S(1)}, bf16[1024,768]{1,0:T(8,128)(2,1)}, u32[]{:S(2)}) copy-start(bf16[1024,768]{1,0:T(8,128)(2,1)} %copy-done.23) | copy-start | bytes 4718596
  301.3 27.6 %collective-permute-start.15 = (f32[96,1536]{1,0:T(8,128)S(1)}, f32[96,1536]{1,0:T(8,128)S(1)}, u32[]{:S(2)}, u32[]{:S(2)}) collective-permute-start(f32[96,1536]{1,0:T(8,128)S(1)} %slice_add_fusion.6), channel_id=1, source_target_pairs={{0,16},{2,18},{4,20},{6,22},{8,24},{10,26},{12,28},{14,30},{16,0},... | collective-permute-start | bytes 1769480 | tf_op jit(solution)/shard_map/ppermute | solution.py:620
  306.2 38.3 %collective-permute-start.14 = (f32[384,768]{1,0:T(8,128)S(1)}, f32[384,768]{1,0:T(8,128)S(1)}, u32[]{:S(2)}, u32[]{:S(2)}) collective-permute-start(f32[384,768]{1,0:T(8,128)S(1)} %convolution_add_fusion.4), channel_id=1, source_target_pairs={{0,4},{2,6},{4,0},{6,2},{8,12},{10,14},{12,8},{14,10},{16,20},{18,... | collective-permute-start | bytes 3538952 | tf_op jit(solution)/shard_map/ppermute | solution.py:620
  322.1 28.1 %copy-start.17 = (f32[192,1152]{1,0:T(8,128)}, f32[192,1152]{1,0:T(8,128)S(1)}, u32[]{:S(2)}) copy-start(f32[192,1152]{1,0:T(8,128)S(1)} %get-tuple-element.212) | copy-start | bytes 2654212
  323.1 5.8 %copy-start.16 = (f32[192,1536]{1,0:T(8,128)S(1)}, f32[192,1536]{1,0:T(8,128)}, u32[]{:S(2)}) copy-start(f32[192,1536]{1,0:T(8,128)} %get-tuple-element.210) | copy-start | bytes 3538948
  323.2 27.0 %collective-permute-start.19 = (f32[208,1152]{1,0:T(8,128)S(1)}, f32[208,1152]{1,0:T(8,128)S(1)}, u32[]{:S(2)}, u32[]{:S(2)}) collective-permute-start(f32[208,1152]{1,0:T(8,128)S(1)} %pad_maximum_fusion.2), channel_id=1, source_target_pairs={{0,8},{2,10},{4,12},{6,14},{8,0},{10,2},{12,4},{14,6},{16,24},{18,... | collective-permute-start | bytes 2875400 | tf_op jit(solution)/shard_map/ppermute | solution.py:620
  348.4 23.8 %collective-permute-start.18 = (f32[192,768]{1,0:T(8,128)}, f32[192,768]{1,0:T(8,128)}, u32[]{:S(2)}, u32[]{:S(2)}) collective-permute-start(f32[192,768]{1,0:T(8,128)} %get-tuple-element.171), channel_id=1, source_target_pairs={{0,8},{2,10},{4,12},{6,14},{8,0},{10,2},{12,4},{14,6},{16,24},{18,... | collective-permute-start | bytes 1769480 | tf_op jit(solution)/shard_map/ppermute | solution.py:620
  351.3 32.5 %collective-permute-start.21 = (f32[112,1152]{1,0:T(8,128)}, f32[112,1152]{1,0:T(8,128)}, u32[]{:S(2)}, u32[]{:S(2)}) collective-permute-start(f32[112,1152]{1,0:T(8,128)} %pad_maximum_fusion.7), channel_id=1, source_target_pairs={{0,16},{2,18},{4,20},{6,22},{8,24},{10,26},{12,28},{14,30},{16,0},... | collective-permute-start | bytes 1548296 | tf_op jit(solution)/shard_map/ppermute | solution.py:620
  360.2 3.3 copy-start.22
  363.4 22.7 %copy-start.18 = (f32[192,1152]{1,0:T(8,128)S(1)}, f32[192,1152]{1,0:T(8,128)}, u32[]{:S(2)}) copy-start(f32[192,1152]{1,0:T(8,128)} %copy-done.17) | copy-start | bytes 2654212
  363.4 36.2 %collective-permute-start.7 = (f32[256,1536]{1,0:T(8,128)S(1)}, f32[256,1536]{1,0:T(8,128)}, u32[]{:S(2)}, u32[]{:S(2)}) collective-permute-start(f32[256,1536]{1,0:T(8,128)S(1)} %copy-done.22), channel_id=1, source_target_pairs={{0,1},{1,0},{2,3},{3,2},{4,5},{5,4},{6,7},{7,6},{8,9},{9,8},{10,11... | collective-permute-start | bytes 4718600 | tf_op jit(solution)/shard_map/ppermute | solution.py:670
  373.2 15.8 %collective-permute-start.20 = (f32[96,768]{1,0:T(8,128)S(1)}, f32[96,768]{1,0:T(8,128)}, u32[]{:S(2)}, u32[]{:S(2)}) collective-permute-start(f32[96,768]{1,0:T(8,128)S(1)} %slice_add_fusion.10), channel_id=1, source_target_pairs={{0,16},{2,18},{4,20},{6,22},{8,24},{10,26},{12,28},{14,30},{16,0},... | collective-permute-start | bytes 884744 | tf_op jit(solution)/shard_map/ppermute | solution.py:620
  402.6 5.5 %collective-permute-start.22 = (f32[64,256]{1,0:T(8,128)S(1)}, f32[64,256]{1,0:T(8,128)S(1)}, u32[]{:S(2)}, u32[]{:S(2)}) collective-permute-start(f32[64,256]{1,0:T(8,128)S(1)} %pad_maximum_fusion.8), channel_id=1, source_target_pairs={{0,1},{1,0},{2,3},{3,2},{4,5},{5,4},{6,7},{7,6},{8,9},{9,8},{10,11... | collective-permute-start | bytes 196616 | tf_op jit(solution)/shard_map/ppermute | solution.py:670
  (14 other events, 21.0 us)
Sparse Core Ops, SparseCore 0:
  122.2 136.9 reduce-scatter.1
where the time goes:
time: 424 us; the launch traced here: 418 us
  Pallas kernels  186 us (44%)
  waiting for transfers between devices  93.4 us (22%)
  matrix products  50 us (12%)
  starting transfers between devices  25.7 us (6%)
  other arithmetic  25.1 us (6%)
  local copies, waits for them, and re-layouts  22.3 us (5%)
  between operations  14.8 us (3%)
    pallas_call x17, Pallas kernels, run_kernel(): pl.pallas_call(kernel, grid=grid, in_specs=specs, out_specs=[pl.BlockSpec...  177 us
    ppermute x12, waiting for transfers between devices, start(): self.came = lax.ppermute(after(self.send, *others), 'dp', pairs)  64.7 us
    dot_general x12, matrix products, mm(): lax.dot_general(a, b, (((1,), (0,)), ((), ())), preferred_element_type=F32)  50 us
    ppermute x10, waiting for transfers between devices, swap_tensor(): return lax.ppermute(values, 'tensor', [(t, t ^ 1) for t in range(n)])  24.1 us
    ppermute x12, starting transfers between devices, start(): self.came = lax.ppermute(after(self.send, *others), 'dp', pairs)  13.5 us
    ppermute x10, starting transfers between devices, swap_tensor(): return lax.ppermute(values, 'tensor', [(t, t ^ 1) for t in range(n)])  12 us
    unnamed x78, local copies, waits for them, and re-layouts  10.2 us
    pallas_call x1, Pallas kernels, product(): pl.pallas_call(kernel, grid=(columns // step,), in_specs=specs, out_specs...  9.59 us
  transfers between devices with their start and end apart: 24, of which 14 were waited for; matrix products, arithmetic and copies ran while one was open for 13% of the time, Pallas kernels for 42%

commit v1 on v0

--- a/solution.py
+++ b/solution.py
@@ -1007,7 +1007,8 @@
 
     def step(sum_of):
         if sum_of.stride < n_dp:
-            sum_of.settle(*order)
+            ends = queue[6:7] if sum_of is near and sum_of.stride == 8 else []
+            sum_of.settle(*order, *ends)
             done = sum_of.stride == n_dp
             order[:] = [sum_of.total if done else sum_of.send]
             if not done:

time: 424 us -> 416 us (0.981)
  waiting for transfers between devices: 93.4 us -> 84.5 us
    ppermute x12, waiting for transfers between devices: 64.7 us -> 53.6 us  [start(): self.came = lax.ppermute(after(self.send, *others), 'dp', pairs)]
    unnamed x78 -> x80, local copies, waits for them, and re-layouts: 10.2 us -> 10.2 us
  transfers between devices with their start and end apart: 24 -> 24, of which waited for: 14 -> 13; matrix products, arithmetic and copies ran while one was open for 13% -> 13% of each run, Pallas kernels for 42% -> 42%
where the time goes in v1:
time: 416 us; the launch traced here: 409 us
  Pallas kernels  186 us (45%)
  waiting for transfers between devices  84.5 us (20%)
  matrix products  50 us (12%)
  starting transfers between devices  27.1 us (7%)
  other arithmetic  23.6 us (6%)
  local copies, waits for them, and re-layouts  22.4 us (5%)
  between operations  14.8 us (4%)
    pallas_call x17, Pallas kernels, run_kernel(): pl.pallas_call(kernel, grid=grid, in_specs=specs, out_specs=[pl.BlockSpec...  177 us
    ppermute x12, waiting for transfers between devices, start(): self.came = lax.ppermute(after(self.send, *others), 'dp', pairs)  53.6 us
    dot_general x12, matrix products, mm(): lax.dot_general(a, b, (((1,), (0,)), ((), ())), preferred_element_type=F32)  50 us
    ppermute x10, waiting for transfers between devices, swap_tensor(): return lax.ppermute(values, 'tensor', [(t, t ^ 1) for t in range(n)])  26.4 us
    ppermute x12, starting transfers between devices, start(): self.came = lax.ppermute(after(self.send, *others), 'dp', pairs)  14.2 us
    ppermute x10, starting transfers between devices, swap_tensor(): return lax.ppermute(values, 'tensor', [(t, t ^ 1) for t in range(n)])  12.8 us
    unnamed x80, local copies, waits for them, and re-layouts  10.2 us
    pallas_call x1, Pallas kernels, product(): pl.pallas_call(kernel, grid=(columns // step,), in_specs=specs, out_specs...  9.8 us
  transfers between devices with their start and end apart: 24, of which 13 were waited for; matrix products, arithmetic and copies ran while one was open for 13% of the time, Pallas kernels for 42%

profile of v1, /device:TPU:14, one launch (start us, length us, event | category | flops | bytes accessed | tf_op | source)
XLA Modules:
  0.0 408.8 jit_solution(18341326251570995120)
XLA Ops:
  7.3 2.7 fusion
  16.9 10.5 %fusion.38.refs_12_.refs_3_.refs_15_ = f32[1024,1536]{1,0:T(8,128)} fusion(bf16[1024,1536]{1,0:T(8,128)(2,1)} %copy-done.3, bf16[1536,1536]{1,0:T(8,128)(2,1)} %refs_2_.15), kind=kOutput, calls=%fused_computation.84 | convolution fusion | flops 4831838208 | bytes 14155776 | tf_op jit(solution)/shard_map/dot_general | solution.py:29
  27.4 6.9 %fusion.37.refs_11_.refs_13_.refs_14_.refs_21_ = f32[1024,1536]{1,0:T(8,128)} fusion(bf16[1024,1536]{1,0:T(8,128)(2,1)S(1)} %copy-done.4, bf16[1536,1536]{1,0:T(8,128)(2,1)S(1)} %bitcast.23), kind=kOutput, calls=%fused_computation.83 | convolution fusion | flops 4831838208 | bytes 14155776 | tf_op jit(solution)/shard_map/dot_general | solution.py:29
  35.6 12.7 %shard_map.279 = (f32[256,1536]{1,0:T(8,128)}, f32[128,1536]{1,0:T(8,128)}, f32[8,1024]{1,0:T(8,128)}, bf16[1536,1024]{1,0:T(8,128)(2,1)}, bf16[1536,1024]{1,0:T(8,128)(2,1)}, /*index=5*/f32[1024,1536]{1,0:T(8,128)}) custom-call(f32[8,1536]{1,0:T(8,128)} %select_maximum_fusion.refs_0_.refs_2_.refs_5_, f32[4,256]{1,0:T(4,128)} %refs_6_.17, ...), custom_call_target="tpu_custom_call" | custom-call | flops 1 | bytes 1 | tf_op jit(solution)/shard_map/pallas_call | solution.py:532
  48.9 13.7 %shard_map.280 = (f32[256,1536]{1,0:T(8,128)}, f32[128,1536]{1,0:T(8,128)}, f32[8,1024]{1,0:T(8,128)}, bf16[1536,1024]{1,0:T(8,128)(2,1)}, bf16[1536,1024]{1,0:T(8,128)(2,1)}, /*index=5*/f32[1024,1536]{1,0:T(8,128)}) custom-call(f32[8,1536]{1,0:T(8,128)} %select_maximum_fusion.refs_0_.ref, ...), custom_call_target="tpu_custom_call", output_to_operand_aliasing={{2}: (16, {}), {3}: (17, {}), {4}: (18, {}), {5}: (19, {})} | custom-call | flops 1 | bytes 1 | tf_op jit(solution)/shard_map/pallas_call | solution.py:532
  62.5 13.7 %shard_map.281 = (f32[256,1536]{1,0:T(8,128)}, f32[128,1536]{1,0:T(8,128)}, f32[8,1024]{1,0:T(8,128)}, bf16[1536,1024]{1,0:T(8,128)(2,1)}, bf16[1536,1024]{1,0:T(8,128)(2,1)}, /*index=5*/f32[1024,1536]{1,0:T(8,128)}) custom-call(f32[8,1536]{1,0:T(8,128)} %select_maximum_fusion.refs_0_.ref, ...), custom_call_target="tpu_custom_call", output_to_operand_aliasing={{2}: (16, {}), {3}: (17, {}), {4}: (18, {}), {5}: (19, {})} | custom-call | flops 1 | bytes 1 | tf_op jit(solution)/shard_map/pallas_call | solution.py:532
  76.3 13.7 %shard_map.282 = (f32[256,1536]{1,0:T(8,128)}, f32[128,1536]{1,0:T(8,128)}, f32[8,1024]{1,0:T(8,128)}, bf16[1536,1024]{1,0:T(8,128)(2,1)}, bf16[1536,1024]{1,0:T(8,128)(2,1)}, /*index=5*/f32[1024,1536]{1,0:T(8,128)}) custom-call(f32[8,1536]{1,0:T(8,128)} %select_maximum_fusion.refs_0_.ref, ...), custom_call_target="tpu_custom_call", output_to_operand_aliasing={{2}: (16, {}), {3}: (17, {}), {4}: (18, {}), {5}: (19, {})} | custom-call | flops 1 | bytes 1 | tf_op jit(solution)/shard_map/pallas_call | solution.py:532
  91.6 2.6 collective-permute-done.refs_1_.refs_20_
  96.8 15.6 %shard_map.287 = (f32[1024,1536]{1,0:T(8,128)}, bf16[1024,1536]{1,0:T(8,128)(2,1)}, bf16[1024,1536]{1,0:T(8,128)(2,1)}) custom-call(f32[8,1024]{1,0:T(8,128)} %get-tuple-element.112.refs_0_.refs_19_, f32[8,1024]{1,0:T(8,128)} %copy-done.19, f32[8,1536]{1,0:T(8,128)} %select_maximum_fusion.refs_0_.refs_2_.refs_5_, ...), custom_call_target="tpu_custom_call" | custom-call | flops 1 | bytes 1 | tf_op jit(solution)/shard_map/pallas_call | solution.py:532
  112.4 9.8 %shard_map.288.refs_2_.refs_24_ = f32[1536,1536]{1,0:T(8,128)} custom-call(bf16[1536,1024]{1,0:T(8,128)(2,1)} %get-tuple-element.123.refs_0_, bf16[1024,1536]{1,0:T(8,128)(2,1)} %get-tuple-element.124.refs_1_), custom_call_target="tpu_custom_call" | custom-call | flops 1 | bytes 1 | tf_op jit(solution)/shard_map/pallas_call | solution.py:595
  122.3 3.1 shard_map.283.refs_5_.refs_3_
  125.4 3.7 collective-permute-done.3.refs_4_.refs_1_
  130.2 2.3 copy-done.6
  132.5 5.0 %fusion.10 = f32[768,1536]{1,0:T(8,128)S(1)} fusion(bf16[1024,1536]{1,0:T(8,128)(2,1)} %shard_map.289.refs_18_, bf16[1536,1024]{1,0:T(8,128)(2,1)S(1)} %copy-done.6), kind=kOutput, calls=%fused_computation.20 | convolution fusion | flops 2415919104 | bytes 9437184 | tf_op jit(solution)/shard_map/dot_general | solution.py:29
  137.6 9.3 %collective-permute-done.5 = f32[768,1536]{1,0:T(8,128)S(1)} collective-permute-done((f32[768,1536]{1,0:T(8,128)S(1)}, f32[768,1536]{1,0:T(8,128)S(1)}, u32[]{:S(2)}, u32[]{:S(2)}) %collective-permute-start.5) | collective-permute-done | bytes 4718624 | tf_op jit(solution)/shard_map/ppermute | solution.py:620
  146.9 2.9 convolution_add_fusion.3.refs_25_
  152.7 19.7 %shard_map.290 = (f32[256,1536]{1,0:T(8,128)}, f32[8,1536]{1,0:T(8,128)}, f32[8,256]{1,0:T(8,128)}, f32[8,1536]{1,0:T(8,128)}, f32[8,128]{1,0:T(8,128)}, /*index...) custom-call(f32[1,1536]{1,0:T(1,128)} %broadcast_in_dim.28.refs_0_, ...), custom_call_target="tpu_custom_call" | custom-call | flops 1 | bytes 1 | tf_op jit(solution)/shard_map/pallas_call | solution.py:532
  173.0 20.7 %shard_map.291 = (f32[256,1536]{1,0:T(8,128)}, f32[8,1536]{1,0:T(8,128)}, f32[8,256]{1,0:T(8,128)}, f32[8,1536]{1,0:T(8,128)}, f32[8,128]{1,0:T(8,128)}, /*index...) custom-call(f32[1,1536]{1,0:T(1,128)} %broadcast_in_dim.28.refs_0_, ...), custom_call_target="tpu_custom_call", output_to_operand_aliasing={{7}: (31, {}), {8}: (32, {})} | custom-call | flops 1 | bytes 1 | tf_op jit(solution)/shard_map/pallas_call | solution.py:532
  196.5 20.8 %shard_map.292 = (f32[256,1536]{1,0:T(8,128)}, f32[8,1536]{1,0:T(8,128)}, f32[8,256]{1,0:T(8,128)}, f32[8,1536]{1,0:T(8,128)}, f32[8,128]{1,0:T(8,128)}, /*index...) custom-call(f32[1,1536]{1,0:T(1,128)} %broadcast_in_dim.28.refs_0_, ...), custom_call_target="tpu_custom_call", output_to_operand_aliasing={{7}: (31, {}), {8}: (32, {})} | custom-call | flops 1 | bytes 1 | tf_op jit(solution)/shard_map/pallas_call | solution.py:532
  217.3 4.4 %convolution_add_fusion.2 = f32[384,1536]{1,0:T(8,128)} fusion(bf16[1024,1536]{1,0:T(8,128)(2,1)S(1)} %copy-done.2, f32[768,1536]{1,0:T(8,128)} %copy-done.34, bf16[1536,1024]{1,0:T(8,128)(2,1)S(1)} %copy-done.6), kind=kOutput, calls=%fused_computation.7 | convolution fusion | flops 1208549376 | bytes 8650752 | tf_op jit(solution)/shard_map/dot_general | solution.py:29
  222.9 21.4 %shard_map.293 = (f32[256,1536]{1,0:T(8,128)}, f32[8,1536]{1,0:T(8,128)}, f32[8,256]{1,0:T(8,128)}, f32[8,1536]{1,0:T(8,128)}, f32[8,128]{1,0:T(8,128)}, /*index...) custom-call(f32[1,1536]{1,0:T(1,128)} %broadcast_in_dim.28.refs_0_, ...), custom_call_target="tpu_custom_call", output_to_operand_aliasing={{7}: (28, {}), {8}: (29, {})} | custom-call | flops 1 | bytes 1 | tf_op jit(solution)/shard_map/pallas_call | solution.py:532
  244.4 3.4 slice_add_fusion
  247.8 6.8 %collective-permute-done.8.refs_1_.refs_2_ = f32[256,1536]{1,0:T(8,128)} collective-permute-done((f32[256,1536]{1,0:T(8,128)}, f32[256,1536]{1,0:T(8,128)}, u32[]{:S(2)}, u32[]{:S(2)}) %collective-permute-start.8) | collective-permute-done | bytes 1572896 | tf_op jit(solution)/shard_map/ppermute | solution.py:670
  257.0 5.2 %fusion.7 = f32[768,1152]{1,0:T(8,128)} fusion(bf16[1536,1024]{1,0:T(8,128)(2,1)S(1)} %copy-done.7, bf16[1024,384]{1,0:T(8,128)(2,1)} %get-tuple-element.159, bf16[1024,768]{1,0:T(8,128)(2,1)S(1)} %slice.277), kind=kOutput, calls=%fused_computation.17 | convolution fusion | flops 1816657920 | bytes 7471104 | tf_op jit(solution)/shard_map/dot_general | solution.py:29
  262.2 2.9 fusion.4
  267.4 4.5 %collective-permute-done.12 = f32[16,1152]{1,0:T(8,128)S(1)} collective-permute-done((f32[16,1152]{1,0:T(8,128)S(1)}, f32[16,1152]{1,0:T(8,128)S(1)}, u32[]{:S(2)}, u32[]{:S(2)}) %collective-permute-start.12) | collective-permute-done | bytes 73760 | tf_op jit(solution)/shard_map/ppermute | solution.py:619
  272.0 3.6 convolution_add_fusion.1
  280.2 2.9 shard_map.295.refs_3_
  283.5 3.2 shard_map.296.refs_3_
  286.7 13.6 %collective-permute-done.13 = f32[192,1536]{1,0:T(8,128)} collective-permute-done((f32[192,1536]{1,0:T(8,128)}, f32[192,1536]{1,0:T(8,128)}, u32[]{:S(2)}, u32[]{:S(2)}) %collective-permute-start.13) | collective-permute-done | bytes 1179680 | tf_op jit(solution)/shard_map/ppermute | solution.py:620
  301.8 2.2 collective-permute-start.15
  304.0 2.0 convolution_add_fusion.4
  307.8 2.7 convolution_add_fusion
  310.5 9.9 %collective-permute-done.16 = f32[400,1152]{1,0:T(8,128)} collective-permute-done((f32[400,1152]{1,0:T(8,128)}, f32[400,1152]{1,0:T(8,128)}, u32[]{:S(2)}, u32[]{:S(2)}) %collective-permute-start.16) | collective-permute-done | bytes 1843232 | tf_op jit(solution)/shard_map/ppermute | solution.py:620
  323.1 2.1 collective-permute-start.19
  325.2 2.0 convolution_add_fusion.5
  330.5 2.0 fusion.25
  332.5 12.3 %collective-permute-done.14 = f32[384,768]{1,0:T(8,128)S(1)} collective-permute-done((f32[384,768]{1,0:T(8,128)S(1)}, f32[384,768]{1,0:T(8,128)S(1)}, u32[]{:S(2)}, u32[]{:S(2)}) %collective-permute-start.14) | collective-permute-done | bytes 1179680 | tf_op jit(solution)/shard_map/ppermute | solution.py:620
  344.9 5.0 %collective-permute-done.17.refs_2_ = f32[256,1536]{1,0:T(8,128)} collective-permute-done((f32[256,1536]{1,0:T(8,128)}, f32[256,1536]{1,0:T(8,128)}, u32[]{:S(2)}, u32[]{:S(2)}) %collective-permute-start.17) | collective-permute-done | bytes 1572896 | tf_op jit(solution)/shard_map/ppermute | solution.py:670
  352.7 2.6 collective-permute-start.21
  355.3 3.1 shard_map.284.refs_5_
  358.4 3.1 shard_map.285.refs_5_
  361.5 3.1 shard_map.286
  364.7 3.0 shard_map.297.refs_3_
  367.7 3.9 collective-permute-done.18
  373.7 8.3 %collective-permute-done.7.refs_2_ = f32[256,1536]{1,0:T(8,128)S(1)} collective-permute-done((f32[256,1536]{1,0:T(8,128)}, f32[256,1536]{1,0:T(8,128)S(1)}, u32[]{:S(2)}, u32[]{:S(2)}) %collective-permute-start.7) | collective-permute-done | bytes 1572896 | tf_op jit(solution)/shard_map/ppermute | solution.py:670
  382.0 3.2 collective-permute-done.21
  395.8 2.9 shard_map.298
  (180 shorter events, 59.0 us)
Async XLA Ops:
  7.2 4.4 %copy-start = (bf16[1024,1536]{1,0:T(8,128)(2,1)S(1)}, bf16[1024,1536]{1,0:T(8,128)(2,1)}, u32[]{:S(2)}) copy-start(bf16[1024,1536]{1,0:T(8,128)(2,1)} %refs_10_.7) | copy-start | bytes 9437188
  7.2 4.4 %copy-start.28 = (f32[1536]{0:T(1024)S(1)}, f32[1536]{0:T(1024)}, u32[]{:S(2)}) copy-start(f32[1536]{0:T(1024)} %param.17) | copy-start | bytes 18436
  7.2 269.8 %reduce-scatter.2.cloned.1.call-start = ((), (), s32[]{:S(2)}) async-start(), calls=%async_computation.1 | async-start | bytes 10027008 | tf_op jit(solution)/shard_map/reduce_scatter | solution.py:988
  15.6 11.8 %slice-start = ((s8[4718592]{0:T(1024)(128)(4,1)}), s8[524288]{0:T(1024)(128)(4,1)S(1)}, s32[]{:S(2)}) async-start(s8[4718592]{0:T(1024)(128)(4,1)} %bitcast.22), calls=%async_computation.2 | async-start | bytes 1048576
  16.9 10.5 %slice-start.1 = ((s8[4718592]{0:T(1024)(128)(4,1)}), s8[4194304]{0:T(1024)(128)(4,1)S(1)}, s32[]{:S(2)}) async-start(s8[4718592]{0:T(1024)(128)(4,1)} %bitcast.22), calls=%async_computation.3 | async-start | bytes 8388608
  16.9 10.5 %copy-start.4 = (bf16[1024,1536]{1,0:T(8,128)(2,1)S(1)}, bf16[1024,1536]{1,0:T(8,128)(2,1)}, u32[]{:S(2)}) copy-start(bf16[1024,1536]{1,0:T(8,128)(2,1)} %copy-done.3) | copy-start | bytes 9437188
  27.4 7.5 %copy-start.29 = (f32[4,1536]{1,0:T(4,128)S(1)}, f32[4,1536]{1,0:T(4,128)}, u32[]{:S(2)}) copy-start(f32[4,1536]{1,0:T(4,128)} %param.22) | copy-start | bytes 73732
  48.3 47.4 %collective-permute-start.4 = (f32[256,1536]{1,0:T(8,128)}, f32[256,1536]{1,0:T(8,128)S(1)}, u32[]{:S(2)}, u32[]{:S(2)}) collective-permute-start(f32[256,1536]{1,0:T(8,128)} %get-tuple-element.119.refs_3_), channel_id=1, source_target_pairs={{0,1},{1,0},{2,3},{3,2},{4,5},{5,4},{6,7},{7,6},{8,9},{9,8},{10,11... | collective-permute-start | bytes 4718600 | tf_op jit(solution)/shard_map/ppermute | solution.py:670
  90.0 4.2 %collective-permute-start = (f32[8,1024]{1,0:T(8,128)}, f32[8,1024]{1,0:T(8,128)S(1)}, u32[]{:S(2)}, u32[]{:S(2)}) collective-permute-start(f32[8,1024]{1,0:T(8,128)} %get-tuple-element.112.refs_0_.refs_19_), channel_id=1, source_target_pairs={{0,1},{1,0},{2,3},{3,2},{4,5},{5,4},{6,7},{7,6},{8,9},{9,8},{10,11... | collective-permute-start | bytes 98312 | tf_op jit(solution)/shard_map/ppermute | solution.py:670
  94.2 34.9 %collective-permute-start.3 = (f32[256,1536]{1,0:T(8,128)}, f32[256,1536]{1,0:T(8,128)S(1)}, u32[]{:S(2)}, u32[]{:S(2)}) collective-permute-start(f32[256,1536]{1,0:T(8,128)} %get-tuple-element.118.refs_3_), channel_id=1, source_target_pairs={{0,1},{1,0},{2,3},{3,2},{4,5},{5,4},{6,7},{7,6},{8,9},{9,8},{10,11... | collective-permute-start | bytes 4718600 | tf_op jit(solution)/shard_map/ppermute | solution.py:670
  130.2 2.3 copy-start.6
  132.5 14.4 %copy-start.1 = (bf16[1024,1536]{1,0:T(8,128)(2,1)S(1)}, bf16[1024,1536]{1,0:T(8,128)(2,1)}, u32[]{:S(2)}) copy-start(bf16[1024,1536]{1,0:T(8,128)(2,1)} %shard_map.289.refs_18_) | copy-start | bytes 9437188
  137.5 13.1 %copy-start.21 = (f32[256,1536]{1,0:T(8,128)S(1)}, f32[256,1536]{1,0:T(8,128)}, u32[]{:S(2)}) copy-start(f32[256,1536]{1,0:T(8,128)} %get-tuple-element.116.refs_3_) | copy-start | bytes 4718596
  137.5 9.4 %collective-permute-start.5 = (f32[768,1536]{1,0:T(8,128)S(1)}, f32[768,1536]{1,0:T(8,128)S(1)}, u32[]{:S(2)}, u32[]{:S(2)}) collective-permute-start(f32[768,1536]{1,0:T(8,128)S(1)} %fusion.10), channel_id=1, source_target_pairs={{0,2},{2,0},{4,6},{6,4},{8,10},{10,8},{12,14},{14,12},{16,18},{18,... | collective-permute-start | bytes 14155784 | tf_op jit(solution)/shard_map/ppermute | solution.py:620
  146.9 3.1 copy-start.34
  150.0 94.4 %collective-permute-start.9 = (f32[384,1536]{1,0:T(8,128)}, f32[384,1536]{1,0:T(8,128)}, u32[]{:S(2)}, u32[]{:S(2)}) collective-permute-start(f32[384,1536]{1,0:T(8,128)} %convolution_add_fusion.3.refs_25_), channel_id=1, source_target_pairs={{0,4},{2,6},{4,0},{6,2},{8,12},{10,14},{12,8},{14,10},{16,20},{18,... | collective-permute-start | bytes 7077896 | tf_op jit(solution)/shard_map/ppermute | solution.py:620
  150.6 44.7 %collective-permute-start.2 = (f32[256,1536]{1,0:T(8,128)S(1)}, f32[256,1536]{1,0:T(8,128)S(1)}, u32[]{:S(2)}, u32[]{:S(2)}) collective-permute-start(f32[256,1536]{1,0:T(8,128)S(1)} %copy-done.21), channel_id=1, source_target_pairs={{0,1},{1,0},{2,3},{3,2},{4,5},{5,4},{6,7},{7,6},{8,9},{9,8},{10,11... | collective-permute-start | bytes 4718600 | tf_op jit(solution)/shard_map/ppermute | solution.py:670
  172.4 49.4 %collective-permute-start.6 = (f32[256,1536]{1,0:T(8,128)}, f32[256,1536]{1,0:T(8,128)S(1)}, u32[]{:S(2)}, u32[]{:S(2)}) collective-permute-start(f32[256,1536]{1,0:T(8,128)} %get-tuple-element.153.refs_1_), channel_id=1, source_target_pairs={{0,1},{1,0},{2,3},{3,2},{4,5},{5,4},{6,7},{7,6},{8,9},{9,8},{10,11... | collective-permute-start | bytes 4718600 | tf_op jit(solution)/shard_map/ppermute | solution.py:670
  193.7 60.9 %collective-permute-start.8 = (f32[256,1536]{1,0:T(8,128)}, f32[256,1536]{1,0:T(8,128)}, u32[]{:S(2)}, u32[]{:S(2)}) collective-permute-start(f32[256,1536]{1,0:T(8,128)} %get-tuple-element.156.refs_1_), channel_id=1, source_target_pairs={{0,1},{1,0},{2,3},{3,2},{4,5},{5,4},{6,7},{7,6},{8,9},{9,8},{10,11... | collective-permute-start | bytes 4718600 | tf_op jit(solution)/shard_map/ppermute | solution.py:670
  196.5 20.8 %copy-start.2 = (bf16[1024,1536]{1,0:T(8,128)(2,1)S(1)}, bf16[1024,1536]{1,0:T(8,128)(2,1)}, u32[]{:S(2)}) copy-start(bf16[1024,1536]{1,0:T(8,128)(2,1)} %shard_map.289.refs_18_) | copy-start | bytes 9437188
  222.9 21.4 %copy-start.20 = (f32[384,1536]{1,0:T(8,128)S(1)}, f32[384,1536]{1,0:T(8,128)}, u32[]{:S(2)}) copy-start(f32[384,1536]{1,0:T(8,128)} %convolution_add_fusion.2) | copy-start | bytes 7077892
  254.6 2.4 copy-start.7
  256.3 5.9 %copy-start.23 = (bf16[1024,768]{1,0:T(8,128)(2,1)}, bf16[1024,768]{1,0:T(8,128)(2,1)S(1)}, u32[]{:S(2)}) copy-start(bf16[1024,768]{1,0:T(8,128)(2,1)S(1)} %slice.277) | copy-start | bytes 4718596
  257.0 5.2 %copy-start.5 = (bf16[1024,1536]{1,0:T(8,128)(2,1)S(1)}, bf16[1024,1536]{1,0:T(8,128)(2,1)}, u32[]{:S(2)}) copy-start(bf16[1024,1536]{1,0:T(8,128)(2,1)} %shard_map.294) | copy-start | bytes 9437188
  262.2 4.1 copy-start.27
  262.2 4.2 %copy-start.32 = (f32[8,256]{1,0:T(8,128)S(1)}, f32[8,256]{1,0:T(8,128)}, u32[]{:S(2)}) copy-start(f32[8,256]{1,0:T(8,128)} %get-tuple-element.162) | copy-start | bytes 24580
  262.2 9.8 %collective-permute-start.11 = (f32[768,1152]{1,0:T(8,128)}, f32[768,1152]{1,0:T(8,128)}, u32[]{:S(2)}, u32[]{:S(2)}) collective-permute-start(f32[768,1152]{1,0:T(8,128)} %fusion.7), channel_id=1, source_target_pairs={{0,2},{2,0},{4,6},{6,4},{8,10},{10,8},{12,14},{14,12},{16,18},{18,... | collective-permute-start | bytes 10616840 | tf_op jit(solution)/shard_map/ppermute | solution.py:620
  265.1 38.9 %collective-permute-start.10 = (f32[768,768]{1,0:T(8,128)}, f32[768,768]{1,0:T(8,128)}, u32[]{:S(2)}, u32[]{:S(2)}) collective-permute-start(f32[768,768]{1,0:T(8,128)} %fusion.4), channel_id=1, source_target_pairs={{0,2},{2,0},{4,6},{6,4},{8,10},{10,8},{12,14},{14,12},{16,18},{18,... | collective-permute-start | bytes 7077896 | tf_op jit(solution)/shard_map/ppermute | solution.py:620
  267.3 4.6 %collective-permute-start.12 = (f32[16,1152]{1,0:T(8,128)S(1)}, f32[16,1152]{1,0:T(8,128)S(1)}, u32[]{:S(2)}, u32[]{:S(2)}) collective-permute-start(f32[16,1152]{1,0:T(8,128)S(1)} %reshape.91), channel_id=1, source_target_pairs={{0,2},{2,0},{4,6},{6,4},{8,10},{10,8},{12,14},{14,12},{16,18},{18,... | collective-permute-start | bytes 221192 | tf_op jit(solution)/shard_map/ppermute | solution.py:619
  271.9 28.4 %collective-permute-start.13 = (f32[192,1536]{1,0:T(8,128)}, f32[192,1536]{1,0:T(8,128)}, u32[]{:S(2)}, u32[]{:S(2)}) collective-permute-start(f32[192,1536]{1,0:T(8,128)} %get-tuple-element.211.refs_2_), channel_id=1, source_target_pairs={{0,8},{2,10},{4,12},{6,14},{8,0},{10,2},{12,4},{14,6},{16,24},{18,... | collective-permute-start | bytes 3538952 | tf_op jit(solution)/shard_map/ppermute | solution.py:620
  277.0 43.3 %collective-permute-start.16 = (f32[400,1152]{1,0:T(8,128)}, f32[400,1152]{1,0:T(8,128)}, u32[]{:S(2)}, u32[]{:S(2)}) collective-permute-start(f32[400,1152]{1,0:T(8,128)} %pad_maximum_fusion.1), channel_id=1, source_target_pairs={{0,4},{2,6},{4,0},{6,2},{8,12},{10,14},{12,8},{14,10},{16,20},{18,... | collective-permute-start | bytes 5529608 | tf_op jit(solution)/shard_map/ppermute | solution.py:620
  278.5 83.0 %collective-permute-start.1 = (f32[256,1536]{1,0:T(8,128)}, f32[256,1536]{1,0:T(8,128)}, u32[]{:S(2)}, u32[]{:S(2)}) collective-permute-start(f32[256,1536]{1,0:T(8,128)} %get-tuple-element.114.refs_3_), channel_id=1, source_target_pairs={{0,1},{1,0},{2,3},{3,2},{4,5},{5,4},{6,7},{7,6},{8,9},{9,8},{10,11... | collective-permute-start | bytes 4718600 | tf_op jit(solution)/shard_map/ppermute | solution.py:670
  283.2 20.8 %copy-start.8 = (bf16[1536,1024]{1,0:T(8,128)(2,1)S(1)}, bf16[1536,1024]{1,0:T(8,128)(2,1)}, u32[]{:S(2)}) copy-start(bf16[1536,1024]{1,0:T(8,128)(2,1)} %get-tuple-element.125) | copy-start | bytes 9437188
  283.2 66.7 %collective-permute-start.17 = (f32[256,1536]{1,0:T(8,128)}, f32[256,1536]{1,0:T(8,128)}, u32[]{:S(2)}, u32[]{:S(2)}) collective-permute-start(f32[256,1536]{1,0:T(8,128)} %get-tuple-element.170.refs_1_), channel_id=1, source_target_pairs={{0,1},{1,0},{2,3},{3,2},{4,5},{5,4},{6,7},{7,6},{8,9},{9,8},{10,11... | collective-permute-start | bytes 4718600 | tf_op jit(solution)/shard_map/ppermute | solution.py:670
  300.3 7.4 %copy-start.11 = (bf16[1024,384]{1,0:T(8,128)(2,1)S(1)}, bf16[1024,384]{1,0:T(8,128)(2,1)}, u32[]{:S(2)}) copy-start(bf16[1024,384]{1,0:T(8,128)(2,1)} %get-tuple-element.159) | copy-start | bytes 2359300
  300.3 7.4 %copy-start.24 = (bf16[1024,768]{1,0:T(8,128)(2,1)S(1)}, bf16[1024,768]{1,0:T(8,128)(2,1)}, u32[]{:S(2)}) copy-start(bf16[1024,768]{1,0:T(8,128)(2,1)} %copy-done.23) | copy-start | bytes 4718596
  301.8 26.9 %collective-permute-start.15 = (f32[96,1536]{1,0:T(8,128)S(1)}, f32[96,1536]{1,0:T(8,128)S(1)}, u32[]{:S(2)}, u32[]{:S(2)}) collective-permute-start(f32[96,1536]{1,0:T(8,128)S(1)} %slice_add_fusion.6), channel_id=1, source_target_pairs={{0,16},{2,18},{4,20},{6,22},{8,24},{10,26},{12,28},{14,30},{16,0},... | collective-permute-start | bytes 1769480 | tf_op jit(solution)/shard_map/ppermute | solution.py:620
  306.0 38.7 %collective-permute-start.14 = (f32[384,768]{1,0:T(8,128)S(1)}, f32[384,768]{1,0:T(8,128)S(1)}, u32[]{:S(2)}, u32[]{:S(2)}) collective-permute-start(f32[384,768]{1,0:T(8,128)S(1)} %convolution_add_fusion.4), channel_id=1, source_target_pairs={{0,4},{2,6},{4,0},{6,2},{8,12},{10,14},{12,8},{14,10},{16,20},{18,... | collective-permute-start | bytes 3538952 | tf_op jit(solution)/shard_map/ppermute | solution.py:620
  322.0 29.5 %copy-start.17 = (f32[192,1152]{1,0:T(8,128)}, f32[192,1152]{1,0:T(8,128)S(1)}, u32[]{:S(2)}) copy-start(f32[192,1152]{1,0:T(8,128)S(1)} %get-tuple-element.212) | copy-start | bytes 2654212
  323.0 7.5 %copy-start.16 = (f32[192,1536]{1,0:T(8,128)S(1)}, f32[192,1536]{1,0:T(8,128)}, u32[]{:S(2)}) copy-start(f32[192,1536]{1,0:T(8,128)} %get-tuple-element.210) | copy-start | bytes 3538948
  323.1 28.5 %collective-permute-start.19 = (f32[208,1152]{1,0:T(8,128)S(1)}, f32[208,1152]{1,0:T(8,128)S(1)}, u32[]{:S(2)}, u32[]{:S(2)}) collective-permute-start(f32[208,1152]{1,0:T(8,128)S(1)} %pad_maximum_fusion.2), channel_id=1, source_target_pairs={{0,8},{2,10},{4,12},{6,14},{8,0},{10,2},{12,4},{14,6},{16,24},{18,... | collective-permute-start | bytes 2875400 | tf_op jit(solution)/shard_map/ppermute | solution.py:620
  328.7 53.4 %collective-permute-start.7 = (f32[256,1536]{1,0:T(8,128)}, f32[256,1536]{1,0:T(8,128)S(1)}, u32[]{:S(2)}, u32[]{:S(2)}) collective-permute-start(f32[256,1536]{1,0:T(8,128)} %get-tuple-element.154.refs_1_), channel_id=1, source_target_pairs={{0,1},{1,0},{2,3},{3,2},{4,5},{5,4},{6,7},{7,6},{8,9},{9,8},{10,11... | collective-permute-start | bytes 4718600 | tf_op jit(solution)/shard_map/ppermute | solution.py:670
  349.9 21.7 %collective-permute-start.18 = (f32[192,768]{1,0:T(8,128)S(1)}, f32[192,768]{1,0:T(8,128)}, u32[]{:S(2)}, u32[]{:S(2)}) collective-permute-start(f32[192,768]{1,0:T(8,128)S(1)} %get-tuple-element.171), channel_id=1, source_target_pairs={{0,8},{2,10},{4,12},{6,14},{8,0},{10,2},{12,4},{14,6},{16,24},{18,... | collective-permute-start | bytes 1769480 | tf_op jit(solution)/shard_map/ppermute | solution.py:620
  352.7 32.5 %collective-permute-start.21 = (f32[112,1152]{1,0:T(8,128)}, f32[112,1152]{1,0:T(8,128)}, u32[]{:S(2)}, u32[]{:S(2)}) collective-permute-start(f32[112,1152]{1,0:T(8,128)} %pad_maximum_fusion.7), channel_id=1, source_target_pairs={{0,16},{2,18},{4,20},{6,22},{8,24},{10,26},{12,28},{14,30},{16,0},... | collective-permute-start | bytes 1548296 | tf_op jit(solution)/shard_map/ppermute | solution.py:620
  364.7 20.5 %copy-start.18 = (f32[192,1152]{1,0:T(8,128)S(1)}, f32[192,1152]{1,0:T(8,128)}, u32[]{:S(2)}) copy-start(f32[192,1152]{1,0:T(8,128)} %copy-done.17) | copy-start | bytes 2654212
  372.6 17.6 %collective-permute-start.20 = (f32[96,768]{1,0:T(8,128)S(1)}, f32[96,768]{1,0:T(8,128)}, u32[]{:S(2)}, u32[]{:S(2)}) collective-permute-start(f32[96,768]{1,0:T(8,128)S(1)} %slice_add_fusion.10), channel_id=1, source_target_pairs={{0,16},{2,18},{4,20},{6,22},{8,24},{10,26},{12,28},{14,30},{16,0},... | collective-permute-start | bytes 884744 | tf_op jit(solution)/shard_map/ppermute | solution.py:620
  382.0 13.8 %copy-start.22 = (f32[256,1536]{1,0:T(8,128)}, f32[256,1536]{1,0:T(8,128)S(1)}, u32[]{:S(2)}) copy-start(f32[256,1536]{1,0:T(8,128)S(1)} %collective-permute-done.7.refs_2_) | copy-start | bytes 4718596
  394.2 5.1 %collective-permute-start.22 = (f32[64,256]{1,0:T(8,128)S(1)}, f32[64,256]{1,0:T(8,128)S(1)}, u32[]{:S(2)}, u32[]{:S(2)}) collective-permute-start(f32[64,256]{1,0:T(8,128)S(1)} %pad_maximum_fusion.8), channel_id=1, source_target_pairs={{0,1},{1,0},{2,3},{3,2},{4,5},{5,4},{6,7},{7,6},{8,9},{9,8},{10,11... | collective-permute-start | bytes 196616 | tf_op jit(solution)/shard_map/ppermute | solution.py:670
  (15 other events, 22.4 us)
Sparse Core Ops, SparseCore 0:
  122.4 136.5 reduce-scatter.1

commit v2 on v1

--- a/solution.py
+++ b/solution.py
@@ -965,7 +965,7 @@
                 given[name] = given[name] + carry[name]
         carry = given
 
-    cut = inner // 2
+    cut = inner // 3
     z_wait = []
     if n_dp > 4:
         z_sum.settle(carry.head_sums)

time: 416 us -> 468 us (1.12)
  waiting for transfers between devices: 84.5 us -> 141 us
    ppermute x12, waiting for transfers between devices: 53.6 us -> 102 us  [start(): self.came = lax.ppermute(after(self.send, *others), 'dp', pairs)]
    ppermute x10, waiting for transfers between devices: 26.4 us -> 39.1 us  [swap_tensor(): return lax.ppermute(values, 'tensor', [(t, t ^ 1) for t in range(n)])]
    unnamed x80 -> x78, local copies, waits for them, and re-layouts: 10.2 us -> 10.4 us
  transfers between devices with their start and end apart: 24 -> 24, of which waited for: 13 -> 11; matrix products, arithmetic and copies ran while one was open for 13% -> 11% of each run, Pallas kernels for 42% -> 32%
where the time goes in v2:
time: 468 us; the launch traced here: 460 us
  Pallas kernels  186 us (40%)
  waiting for transfers between devices  141 us (30%)
  matrix products  50.1 us (11%)
  starting transfers between devices  28.5 us (6%)
  local copies, waits for them, and re-layouts  20.1 us (4%)
  other arithmetic  19.6 us (4%)
  between operations  15.2 us (3%)
    pallas_call x17, Pallas kernels, run_kernel(): pl.pallas_call(kernel, grid=grid, in_specs=specs, out_specs=[pl.BlockSpec...  177 us
    ppermute x12, waiting for transfers between devices, start(): self.came = lax.ppermute(after(self.send, *others), 'dp', pairs)  102 us
    dot_general x12, matrix products, mm(): lax.dot_general(a, b, (((1,), (0,)), ((), ())), preferred_element_type=F32)  50.1 us
    ppermute x10, waiting for transfers between devices, swap_tensor(): return lax.ppermute(values, 'tensor', [(t, t ^ 1) for t in range(n)])  39.1 us
    ppermute x12, starting transfers between devices, start(): self.came = lax.ppermute(after(self.send, *others), 'dp', pairs)  16.8 us
    ppermute x10, starting transfers between devices, swap_tensor(): return lax.ppermute(values, 'tensor', [(t, t ^ 1) for t in range(n)])  11.6 us
    unnamed x78, local copies, waits for them, and re-layouts  10.4 us
    pallas_call x1, Pallas kernels, product(): pl.pallas_call(kernel, grid=(columns // step,), in_specs=specs, out_specs...  9.6 us
  transfers between devices with their start and end apart: 24, of which 11 were waited for; matrix products, arithmetic and copies ran while one was open for 11% of the time, Pallas kernels for 32%

profile of v2, /device:TPU:14, one launch (start us, length us, event | category | flops | bytes accessed | tf_op | source)
XLA Modules:
  0.0 460.4 jit_solution(16859732686977281197)
XLA Ops:
  7.3 2.7 fusion
  12.9 1.8 fusion.18
  16.9 10.5 %fusion.43.refs_12_.refs_3_.refs_15_ = f32[1024,1536]{1,0:T(8,128)} fusion(bf16[1024,1536]{1,0:T(8,128)(2,1)} %copy-done.3, bf16[1536,1536]{1,0:T(8,128)(2,1)} %refs_2_.15), kind=kOutput, calls=%fused_computation.87 | convolution fusion | flops 4831838208 | bytes 14155776 | tf_op jit(solution)/shard_map/dot_general | solution.py:29
  27.4 6.9 %fusion.42.refs_11_.refs_13_.refs_14_.refs_21_ = f32[1024,1536]{1,0:T(8,128)} fusion(bf16[1024,1536]{1,0:T(8,128)(2,1)S(1)} %copy-done.4, bf16[1536,1536]{1,0:T(8,128)(2,1)S(1)} %bitcast.24), kind=kOutput, calls=%fused_computation.86 | convolution fusion | flops 4831838208 | bytes 14155776 | tf_op jit(solution)/shard_map/dot_general | solution.py:29
  35.6 12.7 %shard_map.279 = (f32[256,1536]{1,0:T(8,128)}, f32[128,1536]{1,0:T(8,128)}, f32[8,1024]{1,0:T(8,128)}, bf16[1536,1024]{1,0:T(8,128)(2,1)}, bf16[1536,1024]{1,0:T(8,128)(2,1)}, /*index=5*/f32[1024,1536]{1,0:T(8,128)}) custom-call(f32[8,1536]{1,0:T(8,128)} %select_maximum_fusion.refs_0_.refs_2_.refs_5_, f32[4,256]{1,0:T(4,128)} %refs_6_.17, ...), custom_call_target="tpu_custom_call" | custom-call | flops 1 | bytes 1 | tf_op jit(solution)/shard_map/pallas_call | solution.py:532
  48.9 13.7 %shard_map.280 = (f32[256,1536]{1,0:T(8,128)}, f32[128,1536]{1,0:T(8,128)}, f32[8,1024]{1,0:T(8,128)}, bf16[1536,1024]{1,0:T(8,128)(2,1)}, bf16[1536,1024]{1,0:T(8,128)(2,1)}, /*index=5*/f32[1024,1536]{1,0:T(8,128)}) custom-call(f32[8,1536]{1,0:T(8,128)} %select_maximum_fusion.refs_0_.ref, ...), custom_call_target="tpu_custom_call", output_to_operand_aliasing={{2}: (16, {}), {3}: (17, {}), {4}: (18, {}), {5}: (19, {})} | custom-call | flops 1 | bytes 1 | tf_op jit(solution)/shard_map/pallas_call | solution.py:532
  62.6 13.7 %shard_map.281 = (f32[256,1536]{1,0:T(8,128)}, f32[128,1536]{1,0:T(8,128)}, f32[8,1024]{1,0:T(8,128)}, bf16[1536,1024]{1,0:T(8,128)(2,1)}, bf16[1536,1024]{1,0:T(8,128)(2,1)}, /*index=5*/f32[1024,1536]{1,0:T(8,128)}) custom-call(f32[8,1536]{1,0:T(8,128)} %select_maximum_fusion.refs_0_.ref, ...), custom_call_target="tpu_custom_call", output_to_operand_aliasing={{2}: (16, {}), {3}: (17, {}), {4}: (18, {}), {5}: (19, {})} | custom-call | flops 1 | bytes 1 | tf_op jit(solution)/shard_map/pallas_call | solution.py:532
  76.3 13.7 %shard_map.282 = (f32[256,1536]{1,0:T(8,128)}, f32[128,1536]{1,0:T(8,128)}, f32[8,1024]{1,0:T(8,128)}, bf16[1536,1024]{1,0:T(8,128)(2,1)}, bf16[1536,1024]{1,0:T(8,128)(2,1)}, /*index=5*/f32[1024,1536]{1,0:T(8,128)}) custom-call(f32[8,1536]{1,0:T(8,128)} %select_maximum_fusion.refs_0_.ref, ...), custom_call_target="tpu_custom_call", output_to_operand_aliasing={{2}: (16, {}), {3}: (17, {}), {4}: (18, {}), {5}: (19, {})} | custom-call | flops 1 | bytes 1 | tf_op jit(solution)/shard_map/pallas_call | solution.py:532
  91.5 2.6 collective-permute-done.refs_1_.refs_20_
  95.3 15.6 %shard_map.287 = (f32[1024,1536]{1,0:T(8,128)}, bf16[1024,1536]{1,0:T(8,128)(2,1)}, bf16[1024,1536]{1,0:T(8,128)(2,1)}) custom-call(f32[8,1024]{1,0:T(8,128)} %get-tuple-element.112.refs_0_.refs_19_, f32[8,1024]{1,0:T(8,128)} %copy-done.18, f32[8,1536]{1,0:T(8,128)} %select_maximum_fusion.refs_0_.refs_2_.refs_5_, ...), custom_call_target="tpu_custom_call" | custom-call | flops 1 | bytes 1 | tf_op jit(solution)/shard_map/pallas_call | solution.py:532
  110.9 9.6 %shard_map.288.refs_2_.refs_24_ = f32[1536,1536]{1,0:T(8,128)} custom-call(bf16[1536,1024]{1,0:T(8,128)(2,1)} %get-tuple-element.123.refs_0_, bf16[1024,1536]{1,0:T(8,128)(2,1)} %get-tuple-element.124.refs_1_), custom_call_target="tpu_custom_call" | custom-call | flops 1 | bytes 1 | tf_op jit(solution)/shard_map/pallas_call | solution.py:595
  123.5 3.1 shard_map.283.refs_5_.refs_3_
  126.6 30.1 %collective-permute-done.3.refs_4_.refs_1_ = f32[256,1536]{1,0:T(8,128)S(1)} collective-permute-done((f32[256,1536]{1,0:T(8,128)S(1)}, f32[256,1536]{1,0:T(8,128)S(1)}, u32[]{:S(2)}, u32[]{:S(2)}) %collective-permute-start.3) | collective-permute-done | bytes 1572896 | tf_op jit(solution)/shard_map/ppermute | solution.py:670
  157.8 1.9 copy-done.6
  159.7 4.7 %fusion.16 = f32[768,1536]{1,0:T(8,128)S(1)} fusion(bf16[1024,1536]{1,0:T(8,128)(2,1)} %shard_map.289.refs_18_, bf16[1536,1024]{1,0:T(8,128)(2,1)S(1)} %copy-done.6), kind=kOutput, calls=%fused_computation.22 | convolution fusion | flops 2415919104 | bytes 9437184 | tf_op jit(solution)/shard_map/dot_general | solution.py:29
  164.5 7.9 %collective-permute-done.5 = f32[768,1536]{1,0:T(8,128)S(1)} collective-permute-done((f32[768,1536]{1,0:T(8,128)S(1)}, f32[768,1536]{1,0:T(8,128)S(1)}, u32[]{:S(2)}, u32[]{:S(2)}) %collective-permute-start.5) | collective-permute-done | bytes 4718624 | tf_op jit(solution)/shard_map/ppermute | solution.py:620
  172.4 2.9 convolution_add_fusion.1.refs_25_
  177.8 19.7 %shard_map.290 = (f32[256,1536]{1,0:T(8,128)}, f32[8,1536]{1,0:T(8,128)}, f32[8,256]{1,0:T(8,128)}, f32[8,1536]{1,0:T(8,128)}, f32[8,128]{1,0:T(8,128)}, /*index...) custom-call(f32[1,1536]{1,0:T(1,128)} %broadcast_in_dim.28.refs_0_, ...), custom_call_target="tpu_custom_call" | custom-call | flops 1 | bytes 1 | tf_op jit(solution)/shard_map/pallas_call | solution.py:532
  198.2 20.8 %shard_map.291 = (f32[256,1536]{1,0:T(8,128)}, f32[8,1536]{1,0:T(8,128)}, f32[8,256]{1,0:T(8,128)}, f32[8,1536]{1,0:T(8,128)}, f32[8,128]{1,0:T(8,128)}, /*index...) custom-call(f32[1,1536]{1,0:T(1,128)} %broadcast_in_dim.28.refs_0_, ...), custom_call_target="tpu_custom_call", output_to_operand_aliasing={{7}: (31, {}), {8}: (32, {})} | custom-call | flops 1 | bytes 1 | tf_op jit(solution)/shard_map/pallas_call | solution.py:532
  221.7 21.0 %shard_map.292 = (f32[256,1536]{1,0:T(8,128)}, f32[8,1536]{1,0:T(8,128)}, f32[8,256]{1,0:T(8,128)}, f32[8,1536]{1,0:T(8,128)}, f32[8,128]{1,0:T(8,128)}, /*index...) custom-call(f32[1,1536]{1,0:T(1,128)} %broadcast_in_dim.28.refs_0_, ...), custom_call_target="tpu_custom_call", output_to_operand_aliasing={{7}: (31, {}), {8}: (32, {})} | custom-call | flops 1 | bytes 1 | tf_op jit(solution)/shard_map/pallas_call | solution.py:532
  242.8 4.5 convolution_add_fusion
  248.4 21.2 %shard_map.293 = (f32[256,1536]{1,0:T(8,128)}, f32[8,1536]{1,0:T(8,128)}, f32[8,256]{1,0:T(8,128)}, f32[8,1536]{1,0:T(8,128)}, f32[8,128]{1,0:T(8,128)}, /*index...) custom-call(f32[1,1536]{1,0:T(1,128)} %broadcast_in_dim.28.refs_0_, ...), custom_call_target="tpu_custom_call", output_to_operand_aliasing={{7}: (28, {}), {8}: (29, {})} | custom-call | flops 1 | bytes 1 | tf_op jit(solution)/shard_map/pallas_call | solution.py:532
  269.7 3.4 slice_add_fusion.2
  273.0 6.4 %collective-permute-done.8.refs_1_.refs_2_ = f32[256,1536]{1,0:T(8,128)} collective-permute-done((f32[256,1536]{1,0:T(8,128)}, f32[256,1536]{1,0:T(8,128)}, u32[]{:S(2)}, u32[]{:S(2)}) %collective-permute-start.8) | collective-permute-done | bytes 1572896 | tf_op jit(solution)/shard_map/ppermute | solution.py:670
  280.8 5.4 %fusion.13 = f32[768,896]{1,0:T(8,128)} fusion(bf16[1536,1024]{1,0:T(8,128)(2,1)} %get-tuple-element.125, bf16[1024,384]{1,0:T(8,128)(2,1)} %get-tuple-element.159, bf16[1024,512]{1,0:T(8,128)(2,1)S(1)} %slice.263), kind=kOutput, calls=%fused_computation.19 | convolution fusion | flops 1412956160 | bytes 6160384 | tf_op jit(solution)/shard_map/dot_general | solution.py:29
  286.2 3.4 fusion.5
  292.2 2.9 shard_map.295.refs_3_
  296.8 3.2 shard_map.296.refs_3_
  300.6 17.7 %collective-permute-done.13 = f32[192,1536]{1,0:T(8,128)} collective-permute-done((f32[192,1536]{1,0:T(8,128)}, f32[192,1536]{1,0:T(8,128)}, u32[]{:S(2)}, u32[]{:S(2)}) %collective-permute-start.13) | collective-permute-done | bytes 1179680 | tf_op jit(solution)/shard_map/ppermute | solution.py:620
  319.9 2.6 convolution_add_fusion.3
  326.5 2.8 slice_add_fusion
  329.9 2.3 convolution_add_fusion.2
  332.3 2.4 slice_add_fusion.1
  334.7 23.6 %collective-permute-done.16 = f32[400,896]{1,0:T(8,128)S(1)} collective-permute-done((f32[400,896]{1,0:T(8,128)}, f32[400,896]{1,0:T(8,128)S(1)}, u32[]{:S(2)}, u32[]{:S(2)}) %collective-permute-start.16) | collective-permute-done | bytes 1433632 | tf_op jit(solution)/shard_map/ppermute | solution.py:620
  358.2 2.5 collective-permute-start.15
  361.0 21.0 %collective-permute-done.15 = f32[96,1536]{1,0:T(8,128)S(1)} collective-permute-done((f32[96,1536]{1,0:T(8,128)S(1)}, f32[96,1536]{1,0:T(8,128)S(1)}, u32[]{:S(2)}, u32[]{:S(2)}) %collective-permute-start.15) | collective-permute-done | bytes 589856 | tf_op jit(solution)/shard_map/ppermute | solution.py:620
  383.4 2.0 fusion.31
  385.4 4.5 collective-permute-done.14
  390.6 11.0 %collective-permute-done.19 = f32[208,896]{1,0:T(8,128)S(1)} collective-permute-done((f32[208,896]{1,0:T(8,128)S(1)}, f32[208,896]{1,0:T(8,128)S(1)}, u32[]{:S(2)}, u32[]{:S(2)}) %collective-permute-start.19) | collective-permute-done | bytes 745504 | tf_op jit(solution)/shard_map/ppermute | solution.py:620
  402.6 3.4 collective-permute-start.21
  406.0 3.1 shard_map.284.refs_5_
  409.1 3.1 shard_map.285.refs_5_
  412.2 3.1 shard_map.286
  415.3 2.9 shard_map.297.refs_3_
  418.3 5.6 %collective-permute-done.18 = f32[192,1024]{1,0:T(8,128)S(1)} collective-permute-done((f32[192,1024]{1,0:T(8,128)S(1)}, f32[192,1024]{1,0:T(8,128)S(1)}, u32[]{:S(2)}, u32[]{:S(2)}) %collective-permute-start.18) | collective-permute-done | bytes 786464 | tf_op jit(solution)/shard_map/ppermute | solution.py:620
  424.7 5.6 %collective-permute-start.20 = (f32[96,1024]{1,0:T(8,128)}, f32[96,1024]{1,0:T(8,128)}, u32[]{:S(2)}, u32[]{:S(2)}) collective-permute-start(f32[96,1024]{1,0:T(8,128)} %slice_add_fusion.10), channel_id=1, source_target_pairs={{0,16},{2,18},{4,20},{6,22},{8,24},{10,26},{12,28},{14,30},{16,0},... | collective-permute-start | bytes 1179656 | tf_op jit(solution)/shard_map/ppermute | solution.py:620
  435.3 10.4 %collective-permute-done.20 = f32[96,1024]{1,0:T(8,128)} collective-permute-done((f32[96,1024]{1,0:T(8,128)}, f32[96,1024]{1,0:T(8,128)}, u32[]{:S(2)}, u32[]{:S(2)}) %collective-permute-start.20) | collective-permute-done | bytes 393248 | tf_op jit(solution)/shard_map/ppermute | solution.py:620
  447.6 2.9 shard_map.298
  (178 shorter events, 46.7 us)
Async XLA Ops:
  7.2 4.4 copy-start
  7.2 4.4 copy-start.27
  7.2 316.5 %reduce-scatter.2.cloned.1.call-start = ((), (), s32[]{:S(2)}) async-start(), calls=%async_computation.1 | async-start | bytes 10027008 | tf_op jit(solution)/shard_map/reduce_scatter | solution.py:988
  14.7 2.0 copy-start.30
  14.7 2.0 copy-start.32
  15.6 11.8 %slice-start = ((s8[4718592]{0:T(1024)(128)(4,1)}), s8[524288]{0:T(1024)(128)(4,1)S(1)}, s32[]{:S(2)}) async-start(s8[4718592]{0:T(1024)(128)(4,1)} %bitcast.23), calls=%async_computation.2 | async-start | bytes 1048576
  16.9 10.5 %slice-start.1 = ((s8[4718592]{0:T(1024)(128)(4,1)}), s8[4194304]{0:T(1024)(128)(4,1)S(1)}, s32[]{:S(2)}) async-start(s8[4718592]{0:T(1024)(128)(4,1)} %bitcast.23), calls=%async_computation.3 | async-start | bytes 8388608
  16.9 10.5 %copy-start.4 = (bf16[1024,1536]{1,0:T(8,128)(2,1)S(1)}, bf16[1024,1536]{1,0:T(8,128)(2,1)}, u32[]{:S(2)}) copy-start(bf16[1024,1536]{1,0:T(8,128)(2,1)} %copy-done.3) | copy-start | bytes 9437188
  27.4 7.5 %copy-start.28 = (f32[4,1536]{1,0:T(4,128)S(1)}, f32[4,1536]{1,0:T(4,128)}, u32[]{:S(2)}) copy-start(f32[4,1536]{1,0:T(4,128)} %param.22) | copy-start | bytes 73732
  48.4 45.8 %collective-permute-start.4 = (f32[256,1536]{1,0:T(8,128)}, f32[256,1536]{1,0:T(8,128)S(1)}, u32[]{:S(2)}, u32[]{:S(2)}) collective-permute-start(f32[256,1536]{1,0:T(8,128)} %get-tuple-element.119.refs_3_), channel_id=1, source_target_pairs={{0,1},{1,0},{2,3},{3,2},{4,5},{5,4},{6,7},{7,6},{8,9},{9,8},{10,11... | collective-permute-start | bytes 4718600 | tf_op jit(solution)/shard_map/ppermute | solution.py:670
  90.0 4.2 collective-permute-start
  121.9 34.7 %collective-permute-start.3 = (f32[256,1536]{1,0:T(8,128)S(1)}, f32[256,1536]{1,0:T(8,128)S(1)}, u32[]{:S(2)}, u32[]{:S(2)}) collective-permute-start(f32[256,1536]{1,0:T(8,128)S(1)} %copy-done.20), channel_id=1, source_target_pairs={{0,1},{1,0},{2,3},{3,2},{4,5},{5,4},{6,7},{7,6},{8,9},{9,8},{10,11... | collective-permute-start | bytes 4718600 | tf_op jit(solution)/shard_map/ppermute | solution.py:670
  159.7 12.7 %copy-start.1 = (bf16[1024,1536]{1,0:T(8,128)(2,1)S(1)}, bf16[1024,1536]{1,0:T(8,128)(2,1)}, u32[]{:S(2)}) copy-start(bf16[1024,1536]{1,0:T(8,128)(2,1)} %shard_map.289.refs_18_) | copy-start | bytes 9437188
  164.4 11.4 %copy-start.21 = (f32[256,1536]{1,0:T(8,128)S(1)}, f32[256,1536]{1,0:T(8,128)}, u32[]{:S(2)}) copy-start(f32[256,1536]{1,0:T(8,128)} %get-tuple-element.116.refs_3_) | copy-start | bytes 4718596
  164.4 8.0 %collective-permute-start.5 = (f32[768,1536]{1,0:T(8,128)S(1)}, f32[768,1536]{1,0:T(8,128)S(1)}, u32[]{:S(2)}, u32[]{:S(2)}) collective-permute-start(f32[768,1536]{1,0:T(8,128)S(1)} %fusion.16), channel_id=1, source_target_pairs={{0,2},{2,0},{4,6},{6,4},{8,10},{10,8},{12,14},{14,12},{16,18},{18,... | collective-permute-start | bytes 14155784 | tf_op jit(solution)/shard_map/ppermute | solution.py:620
  172.4 2.9 copy-start.33
  175.2 94.4 %collective-permute-start.9 = (f32[384,1536]{1,0:T(8,128)}, f32[384,1536]{1,0:T(8,128)}, u32[]{:S(2)}, u32[]{:S(2)}) collective-permute-start(f32[384,1536]{1,0:T(8,128)} %convolution_add_fusion.1.refs_25_), channel_id=1, source_target_pairs={{0,4},{2,6},{4,0},{6,2},{8,12},{10,14},{12,8},{14,10},{16,20},{18,... | collective-permute-start | bytes 7077896 | tf_op jit(solution)/shard_map/ppermute | solution.py:620
  175.8 44.7 %collective-permute-start.2 = (f32[256,1536]{1,0:T(8,128)S(1)}, f32[256,1536]{1,0:T(8,128)S(1)}, u32[]{:S(2)}, u32[]{:S(2)}) collective-permute-start(f32[256,1536]{1,0:T(8,128)S(1)} %copy-done.21), channel_id=1, source_target_pairs={{0,1},{1,0},{2,3},{3,2},{4,5},{5,4},{6,7},{7,6},{8,9},{9,8},{10,11... | collective-permute-start | bytes 4718600 | tf_op jit(solution)/shard_map/ppermute | solution.py:670
  197.6 49.7 %collective-permute-start.6 = (f32[256,1536]{1,0:T(8,128)}, f32[256,1536]{1,0:T(8,128)S(1)}, u32[]{:S(2)}, u32[]{:S(2)}) collective-permute-start(f32[256,1536]{1,0:T(8,128)} %get-tuple-element.153.refs_1_), channel_id=1, source_target_pairs={{0,1},{1,0},{2,3},{3,2},{4,5},{5,4},{6,7},{7,6},{8,9},{9,8},{10,11... | collective-permute-start | bytes 4718600 | tf_op jit(solution)/shard_map/ppermute | solution.py:670
  218.9 60.5 %collective-permute-start.8 = (f32[256,1536]{1,0:T(8,128)}, f32[256,1536]{1,0:T(8,128)}, u32[]{:S(2)}, u32[]{:S(2)}) collective-permute-start(f32[256,1536]{1,0:T(8,128)} %get-tuple-element.156.refs_1_), channel_id=1, source_target_pairs={{0,1},{1,0},{2,3},{3,2},{4,5},{5,4},{6,7},{7,6},{8,9},{9,8},{10,11... | collective-permute-start | bytes 4718600 | tf_op jit(solution)/shard_map/ppermute | solution.py:670
  221.7 21.1 %copy-start.2 = (bf16[1024,1536]{1,0:T(8,128)(2,1)S(1)}, bf16[1024,1536]{1,0:T(8,128)(2,1)}, u32[]{:S(2)}) copy-start(bf16[1024,1536]{1,0:T(8,128)(2,1)} %shard_map.289.refs_18_) | copy-start | bytes 9437188
  248.4 21.3 %copy-start.19 = (f32[384,1536]{1,0:T(8,128)S(1)}, f32[384,1536]{1,0:T(8,128)}, u32[]{:S(2)}) copy-start(f32[384,1536]{1,0:T(8,128)} %convolution_add_fusion) | copy-start | bytes 7077892
  280.7 5.4 %copy-start.22 = (bf16[1024,512]{1,0:T(8,128)(2,1)}, bf16[1024,512]{1,0:T(8,128)(2,1)S(1)}, u32[]{:S(2)}) copy-start(bf16[1024,512]{1,0:T(8,128)(2,1)S(1)} %slice.263) | copy-start | bytes 3145732
  280.7 5.5 %copy-start.5 = (bf16[1024,1536]{1,0:T(8,128)(2,1)S(1)}, bf16[1024,1536]{1,0:T(8,128)(2,1)}, u32[]{:S(2)}) copy-start(bf16[1024,1536]{1,0:T(8,128)(2,1)} %shard_map.294) | copy-start | bytes 9437188
  280.7 5.5 %copy-start.7 = (bf16[1536,1024]{1,0:T(8,128)(2,1)S(1)}, bf16[1536,1024]{1,0:T(8,128)(2,1)}, u32[]{:S(2)}) copy-start(bf16[1536,1024]{1,0:T(8,128)(2,1)} %get-tuple-element.125) | copy-start | bytes 9437188
  286.1 5.0 %copy-start.26 = (f32[8,1536]{1,0:T(8,128)S(1)}, f32[8,1536]{1,0:T(8,128)}, u32[]{:S(2)}) copy-start(f32[8,1536]{1,0:T(8,128)} %get-tuple-element.160) | copy-start | bytes 147460
  286.1 5.1 %copy-start.31 = (f32[8,256]{1,0:T(8,128)S(1)}, f32[8,256]{1,0:T(8,128)}, u32[]{:S(2)}) copy-start(f32[8,256]{1,0:T(8,128)} %get-tuple-element.162) | copy-start | bytes 24580
  286.1 33.8 %collective-permute-start.11 = (f32[768,896]{1,0:T(8,128)}, f32[768,896]{1,0:T(8,128)}, u32[]{:S(2)}, u32[]{:S(2)}) collective-permute-start(f32[768,896]{1,0:T(8,128)} %fusion.13), channel_id=1, source_target_pairs={{0,2},{2,0},{4,6},{6,4},{8,10},{10,8},{12,14},{14,12},{16,18},{18,... | collective-permute-start | bytes 8257544 | tf_op jit(solution)/shard_map/ppermute | solution.py:620
  289.7 36.8 %collective-permute-start.10 = (f32[768,1024]{1,0:T(8,128)}, f32[768,1024]{1,0:T(8,128)}, u32[]{:S(2)}, u32[]{:S(2)}) collective-permute-start(f32[768,1024]{1,0:T(8,128)} %fusion.5), channel_id=1, source_target_pairs={{0,2},{2,0},{4,6},{6,4},{8,10},{10,8},{12,14},{14,12},{16,18},{18,... | collective-permute-start | bytes 9437192 | tf_op jit(solution)/shard_map/ppermute | solution.py:620
  290.1 28.2 %collective-permute-start.13 = (f32[192,1536]{1,0:T(8,128)}, f32[192,1536]{1,0:T(8,128)}, u32[]{:S(2)}, u32[]{:S(2)}) collective-permute-start(f32[192,1536]{1,0:T(8,128)} %get-tuple-element.198.refs_2_), channel_id=1, source_target_pairs={{0,8},{2,10},{4,12},{6,14},{8,0},{10,2},{12,4},{14,6},{16,24},{18,... | collective-permute-start | bytes 3538952 | tf_op jit(solution)/shard_map/ppermute | solution.py:620
  292.1 7.9 %collective-permute-start.12 = (f32[16,896]{1,0:T(8,128)S(1)}, f32[16,896]{1,0:T(8,128)S(1)}, u32[]{:S(2)}, u32[]{:S(2)}) collective-permute-start(f32[16,896]{1,0:T(8,128)S(1)} %reshape.82), channel_id=1, source_target_pairs={{0,2},{2,0},{4,6},{6,4},{8,10},{10,8},{12,14},{14,12},{16,18},{18,... | collective-permute-start | bytes 172040 | tf_op jit(solution)/shard_map/ppermute | solution.py:619
  295.1 24.8 %copy-start.11 = (bf16[1024,384]{1,0:T(8,128)(2,1)S(1)}, bf16[1024,384]{1,0:T(8,128)(2,1)}, u32[]{:S(2)}) copy-start(bf16[1024,384]{1,0:T(8,128)(2,1)} %get-tuple-element.159) | copy-start | bytes 2359300
  295.1 24.8 %copy-start.23 = (bf16[1024,512]{1,0:T(8,128)(2,1)S(1)}, bf16[1024,512]{1,0:T(8,128)(2,1)}, u32[]{:S(2)}) copy-start(bf16[1024,512]{1,0:T(8,128)(2,1)} %copy-done.22) | copy-start | bytes 3145732
  295.1 117.0 %collective-permute-start.1 = (f32[256,1536]{1,0:T(8,128)}, f32[256,1536]{1,0:T(8,128)}, u32[]{:S(2)}, u32[]{:S(2)}) collective-permute-start(f32[256,1536]{1,0:T(8,128)} %get-tuple-element.114.refs_3_), channel_id=1, source_target_pairs={{0,1},{1,0},{2,3},{3,2},{4,5},{5,4},{6,7},{7,6},{8,9},{9,8},{10,11... | collective-permute-start | bytes 4718600 | tf_op jit(solution)/shard_map/ppermute | solution.py:670
  300.0 90.1 %collective-permute-start.17 = (f32[256,1536]{1,0:T(8,128)}, f32[256,1536]{1,0:T(8,128)}, u32[]{:S(2)}, u32[]{:S(2)}) collective-permute-start(f32[256,1536]{1,0:T(8,128)} %get-tuple-element.170.refs_1_), channel_id=1, source_target_pairs={{0,1},{1,0},{2,3},{3,2},{4,5},{5,4},{6,7},{7,6},{8,9},{9,8},{10,11... | collective-permute-start | bytes 4718600 | tf_op jit(solution)/shard_map/ppermute | solution.py:670
  318.4 111.9 %collective-permute-start.7 = (f32[256,1536]{1,0:T(8,128)}, f32[256,1536]{1,0:T(8,128)}, u32[]{:S(2)}, u32[]{:S(2)}) collective-permute-start(f32[256,1536]{1,0:T(8,128)} %get-tuple-element.154.refs_1_), channel_id=1, source_target_pairs={{0,1},{1,0},{2,3},{3,2},{4,5},{5,4},{6,7},{7,6},{8,9},{9,8},{10,11... | collective-permute-start | bytes 4718600 | tf_op jit(solution)/shard_map/ppermute | solution.py:670
  323.7 34.6 %collective-permute-start.16 = (f32[400,896]{1,0:T(8,128)}, f32[400,896]{1,0:T(8,128)S(1)}, u32[]{:S(2)}, u32[]{:S(2)}) collective-permute-start(f32[400,896]{1,0:T(8,128)} %pad_maximum_fusion.1), channel_id=1, source_target_pairs={{0,4},{2,6},{4,0},{6,2},{8,12},{10,14},{12,8},{14,10},{16,20},{18,... | collective-permute-start | bytes 4300808 | tf_op jit(solution)/shard_map/ppermute | solution.py:620
  326.5 3.4 copy-start.8
  326.5 3.4 copy-start.12
  326.5 3.4 copy-start.24
  329.3 60.5 %collective-permute-start.14 = (f32[384,1024]{1,0:T(8,128)S(1)}, f32[384,1024]{1,0:T(8,128)S(1)}, u32[]{:S(2)}, u32[]{:S(2)}) collective-permute-start(f32[384,1024]{1,0:T(8,128)S(1)} %slice_add_fusion), channel_id=1, source_target_pairs={{0,4},{2,6},{4,0},{6,2},{8,12},{10,14},{12,8},{14,10},{16,20},{18,... | collective-permute-start | bytes 4718600 | tf_op jit(solution)/shard_map/ppermute | solution.py:620
  334.7 48.7 %copy-start.17 = (f32[192,1536]{1,0:T(8,128)S(1)}, f32[192,1536]{1,0:T(8,128)}, u32[]{:S(2)}) copy-start(f32[192,1536]{1,0:T(8,128)} %get-tuple-element.197) | copy-start | bytes 3538948
  358.2 23.8 %collective-permute-start.15 = (f32[96,1536]{1,0:T(8,128)S(1)}, f32[96,1536]{1,0:T(8,128)S(1)}, u32[]{:S(2)}, u32[]{:S(2)}) collective-permute-start(f32[96,1536]{1,0:T(8,128)S(1)} %slice_add_fusion.9), channel_id=1, source_target_pairs={{0,16},{2,18},{4,20},{6,22},{8,24},{10,26},{12,28},{14,30},{16,0},... | collective-permute-start | bytes 1769480 | tf_op jit(solution)/shard_map/ppermute | solution.py:620
  382.0 19.5 %collective-permute-start.19 = (f32[208,896]{1,0:T(8,128)S(1)}, f32[208,896]{1,0:T(8,128)S(1)}, u32[]{:S(2)}, u32[]{:S(2)}) collective-permute-start(f32[208,896]{1,0:T(8,128)S(1)} %pad_maximum_fusion.2), channel_id=1, source_target_pairs={{0,8},{2,10},{4,12},{6,14},{8,0},{10,2},{12,4},{14,6},{16,24},{18,... | collective-permute-start | bytes 2236424 | tf_op jit(solution)/shard_map/ppermute | solution.py:620
  390.2 33.7 %collective-permute-start.18 = (f32[192,1024]{1,0:T(8,128)S(1)}, f32[192,1024]{1,0:T(8,128)S(1)}, u32[]{:S(2)}, u32[]{:S(2)}) collective-permute-start(f32[192,1024]{1,0:T(8,128)S(1)} %get-tuple-element.171), channel_id=1, source_target_pairs={{0,8},{2,10},{4,12},{6,14},{8,0},{10,2},{12,4},{14,6},{16,24},{18,... | collective-permute-start | bytes 2359304 | tf_op jit(solution)/shard_map/ppermute | solution.py:620
  402.6 27.7 %collective-permute-start.21 = (f32[112,896]{1,0:T(8,128)}, f32[112,896]{1,0:T(8,128)S(1)}, u32[]{:S(2)}, u32[]{:S(2)}) collective-permute-start(f32[112,896]{1,0:T(8,128)} %pad_maximum_fusion.7), channel_id=1, source_target_pairs={{0,16},{2,18},{4,20},{6,22},{8,24},{10,26},{12,28},{14,30},{16,0},... | collective-permute-start | bytes 1204232 | tf_op jit(solution)/shard_map/ppermute | solution.py:620
  424.7 21.0 %collective-permute-start.20 = (f32[96,1024]{1,0:T(8,128)}, f32[96,1024]{1,0:T(8,128)}, u32[]{:S(2)}, u32[]{:S(2)}) collective-permute-start(f32[96,1024]{1,0:T(8,128)} %slice_add_fusion.10), channel_id=1, source_target_pairs={{0,16},{2,18},{4,20},{6,22},{8,24},{10,26},{12,28},{14,30},{16,0},... | collective-permute-start | bytes 1179656 | tf_op jit(solution)/shard_map/ppermute | solution.py:620
  434.2 16.4 %collective-permute-start.22 = (f32[64,256]{1,0:T(8,128)S(1)}, f32[64,256]{1,0:T(8,128)S(1)}, u32[]{:S(2)}, u32[]{:S(2)}) collective-permute-start(f32[64,256]{1,0:T(8,128)S(1)} %pad_maximum_fusion.8), channel_id=1, source_target_pairs={{0,1},{1,0},{2,3},{3,2},{4,5},{5,4},{6,7},{7,6},{8,9},{9,8},{10,11... | collective-permute-start | bytes 196616 | tf_op jit(solution)/shard_map/ppermute | solution.py:670
  (14 other events, 19.4 us)
Sparse Core Ops, SparseCore 0:
  120.7 129.0 reduce-scatter.1
